TPU v7x, 128 devices: a whole 4x4x4 slice. The times are simulated.
128 devices in a mesh: lb: 16 (over z_lo, y, core), rb: 8 (over x, z_hi).
Axes of the slice: x: 4, y: 4, z: 4 (z_hi: 2, z_lo: 2; z = z_hi * 2 + z_lo), core: 2. Of those that a mesh axis runs over, the one named last changes fastest.
Arguments:
- wavefunction: bfloat16 [3072, 4, 3072], P('lb', None, 'rb'), may hold values from -6 to 6
- left_environment: bfloat16 [8, 2048, 3072], P(None, 'lb'), may hold values from -0.109375 to 0.109375
- operator_left: float32 [8, 8, 2, 2], replicated, may hold values from -1.5 to 1.5
- operator_right: float32 [8, 8, 2, 2], replicated, may hold values from -1.5 to 1.5
- right_environment: bfloat16 [8, 3072, 3072], P(None, 'rb', 'lb'), may hold values from -0.0546875 to 0.0546875
- row_sector: int32 [16], replicated, may hold values from 0 to 7, never falling along the last dimension, each value on 1 to 4 neighbouring positions
Outputs:
- applied_state: bfloat16 [2048, 4, 3072], P('lb', None, 'rb')
- density: float32 [2048, 2048], P('lb', 'rb')
Inputs may be any that keep to these rules, and one draw needn't show every extreme that they name: `row_sector`: entry t is the sector of output rows t * 128 to (t + 1) * 128 - 1. Entries never fall along t; each sector holds 1 to 4 tiles, and one holds exactly 4.
All inputs are finite; a program needn't handle non-finite values.
Results may differ from a plain program's by a relative error of at most 0.013.
Values may be sent and summed in bfloat16 or wider, within the bound.
A program may use at most 128 MiB of HBM per device.

v0:
```python
import math

import jax
import jax.numpy as jnp
from jax import lax
from jax.sharding import Mesh
from jax.sharding import PartitionSpec as P

BOND_WIDTH = 3072
SECTOR_TILES = 4
RB = ("rb_0", "rb_1")


def shifted(value, axis, by):
    devices = lax.axis_size(axis)
    pairs = [(i, i + by) for i in range(devices) if 0 <= i + by < devices]
    return lax.ppermute(value, axis, pairs)


def summed_rows(value, axes, dim):
    for axis in axes:
        value = lax.psum_scatter(value, axis, scatter_dimension=dim, tiled=True)
    return value


def split_up(value, dim, devices):
    before, after = (value.shape[:dim], value.shape[dim + 1 :])
    return jnp.moveaxis(value.reshape(*before, devices, -1, *after), dim, 0)


def sent_and_summed(value, axis, dim):
    parts = split_up(value, dim, lax.axis_size(axis))
    arrived = lax.all_to_all(parts, axis, split_axis=0, concat_axis=0, tiled=True)
    return arrived.astype(jnp.float32).sum(axis=0)


def combine_operators(operator_left, operator_right):
    channels = operator_left.shape[0]
    joined = jnp.einsum(
        "aups,uvqt->avpqst", operator_left, operator_right, precision=lax.Precision.HIGHEST
    )
    return joined.reshape(channels, channels, 4, 4)


def label_at(labels, position):
    matches = jnp.arange(labels.shape[0], dtype=jnp.int32) == position
    return (jnp.sum(jnp.where(matches, labels, 0)), jnp.any(matches))


def tile_gram(left_tile, right_tile):
    return lax.dot_general(
        left_tile, right_tile, (((1,), (1,)), ((), ())), preferred_element_type=jnp.float32
    )


def fetch_tile(own_tile, offset):
    return shifted(own_tile, "lb", -offset)


def shards(
    wavefunction, left_environment, operator_left, operator_right, right_environment, row_sector
):
    channels, row_count, full_bond = left_environment.shape
    local_right = wavefunction.shape[2]
    left_matrix = left_environment.reshape(channels * row_count, full_bond)
    rows_piece = lax.all_gather(wavefunction, "lb", axis=0, tiled=True)
    flat_piece = rows_piece.reshape(rows_piece.shape[0], 4 * local_right)
    left_part = jnp.dot(left_matrix, flat_piece, preferred_element_type=jnp.float32)
    left_part = left_part.reshape(channels, row_count, 4, local_right)
    combined = combine_operators(operator_left, operator_right)
    mixed_part = jnp.einsum(
        "avyx,alxr->lyvr", combined, left_part, precision=lax.Precision.HIGHEST
    ).astype(jnp.bfloat16)
    mixed_matrix = mixed_part.reshape(row_count * 4, channels * local_right)
    columns_piece = lax.all_gather(right_environment, "lb", axis=2, tiled=True)
    flat_piece = columns_piece.reshape(channels * local_right, columns_piece.shape[2])
    partial_value = jnp.dot(mixed_matrix, flat_piece, preferred_element_type=jnp.float32)
    summed = summed_rows(partial_value.astype(jnp.bfloat16), RB, 1).astype(jnp.float32)
    applied = summed.astype(jnp.bfloat16).reshape(row_count, 4, summed.shape[1])
    own_tile = applied.reshape(row_count, 4 * summed.shape[1])
    own_index = lax.axis_index("lb")
    tile_count = lax.axis_size("lb")
    reach_tiles = SECTOR_TILES - 1
    own_label = label_at(row_sector, own_index)[0]
    buffer = jnp.zeros((row_count, (tile_count + 2 * reach_tiles) * row_count), jnp.float32)

    def place_block(buffer, gram_block, offset):
        mate_index = own_index + offset
        mate_label, inside = label_at(row_sector, mate_index)
        keep_block = jnp.logical_and(inside, mate_label == own_label)
        gram_block = jnp.where(keep_block, gram_block, jnp.float32(0.0))
        column_start = (mate_index + reach_tiles) * row_count
        return lax.dynamic_update_slice(buffer, gram_block, (jnp.int32(0), column_start))

    buffer = place_block(buffer, tile_gram(own_tile, own_tile), 0)
    for distance in range(1, SECTOR_TILES):
        gram_block = tile_gram(own_tile, fetch_tile(own_tile, distance))
        buffer = place_block(buffer, gram_block, distance)
        returned = shifted(gram_block.astype(jnp.bfloat16), "lb", distance).astype(gram_block.dtype)
        buffer = place_block(buffer, returned.T, -distance)
    full_rows = buffer[:, reach_tiles * row_count : (reach_tiles + tile_count) * row_count]
    density = sent_and_summed(full_rows.astype(jnp.bfloat16), RB, 1) * (
        1.0 / math.sqrt(4.0 * BOND_WIDTH)
    )
    return (applied, density)


def solution(mesh):
    torus = Mesh(mesh.devices.reshape(mesh.shape["lb"], 4, 2), ("lb", "rb_0", "rb_1"))
    in_specs = (P("lb", None, RB), P(None, "lb", None), P(), P(), P(None, RB, "lb"), P())
    out_specs = (P("lb", None, RB), P("lb", RB))
    return jax.shard_map(
        shards, mesh=torus, in_specs=in_specs, out_specs=out_specs, check_vma=False
    )
```

profile of v0, /device:TPU:9, one launch (start us, length us, event | category | flops | bytes accessed | tf_op | source)
XLA Modules:
  0.0 338.7 jit_solution(16183151076118569877)
XLA Ops:
  7.2 0.7 all-gather.3.cloned.1.call-update
  8.0 3.0 copy.27
  11.0 1.1 convolution_bitcast_fusion
  12.2 0.7 copy.25
  12.9 56.5 %all-gather.3.cloned.1.call-done = bf16[3072,4,384]{2,1,0:T(4,128)(2,1)} async-done(((bf16[192,4,384]{2,1,0:T(4,128)(2,1)}), bf16[3072,4,384]{2,1,0:T(4,128)(2,1)}) %all-gather.3.cloned.1.call-update) | async-done | bytes 9437200 | tf_op jit(solution)/shard_map/all_gather | solution.py:66
  69.4 15.5 %copy.41 = bf16[3072,4,384]{0,2,1:T(8,128)(2,1)} copy(bf16[3072,4,384]{2,1,0:T(4,128)(2,1)} %all-gather.3.cloned.1.call-done) | data formatting | bytes 18874368 | tf_op jit(solution)/shard_map/reshape | solution.py:67
  84.9 15.2 %fusion = f32[8,128,4,384]{3,0,2,1:T(8,128)S(1)} fusion(bf16[3072,4,384]{0,2,1:T(8,128)(2,1)} %copy.41, bf16[8,128,3072,1]{2,1,0,3:T(8,128)(2,1)} %bitcast.62), kind=kOutput, calls=%fused_computation | convolution fusion | flops 9663676416 | bytes 22020096 | tf_op jit(solution)/shard_map/dot_general | solution.py:68
  100.1 5.7 %bitcast_convert_fusion = bf16[128,384,8,4]{1,2,3,0:T(8,128)(2,1)S(1)} fusion(f32[8,8,4,4,1]{1,0,3,2,4:T(8,128)S(1)} %bitcast.60, f32[8,128,4,384]{3,0,2,1:T(8,128)S(1)} %fusion), kind=kOutput, calls=%fused_computation.4 | convolution fusion | flops 605552640 | bytes 9441280 | tf_op jit(solution)/shard_map/avyx,alxr->lyvr/dot_general | solution.py:71
  105.8 0.7 copy.49
  106.5 66.9 %all-gather.5.cloned.1.call-done = bf16[8,384,3072]{1,0,2:T(8,128)(2,1)} async-done(((bf16[8,384,192]{1,0,2:T(8,128)(2,1)}), bf16[8,384,3072]{1,0,2:T(8,128)(2,1)}) %all-gather.5.cloned.1.call-update) | async-done | bytes 18874384 | tf_op jit(solution)/shard_map/all_gather | solution.py:75
  173.4 24.0 %copy.28 = bf16[8,384,3072]{2,1,0:T(8,128)(2,1)} copy(bf16[8,384,3072]{1,0,2:T(8,128)(2,1)} %all-gather.5.cloned.1.call-done) | data formatting | bytes 37748736 | tf_op jit(solution)/shard_map/all_gather | solution.py:75
  197.4 15.1 %convolution_convert_fusion = bf16[512,3072]{1,0:T(8,128)(2,1)} fusion(bf16[512,3072]{1,0:T(8,128)(2,1)S(1)} %bitcast.57, bf16[3072,3072]{1,0:T(8,128)(2,1)} %bitcast.55), kind=kOutput, calls=%fused_computation.6 | convolution fusion | flops 9665249280 | bytes 25165824 | tf_op jit(solution)/shard_map/dot_general | solution.py:77
  212.6 38.9 %reduce-scatter.5.cloned.1.call-done = bf16[512,768]{1,0:T(8,128)(2,1)} async-done(((bf16[512,3072]{1,0:T(8,128)(2,1)}), bf16[512,768]{1,0:T(8,128)(2,1)}) %reduce-scatter.5.cloned.1.call-update) | async-done | bytes 786448 | tf_op jit(solution)/shard_map/reduce_scatter | solution.py:22
  251.5 2.3 copy.47
  253.8 21.5 %reduce-scatter.7.cloned.1.call-done = bf16[384,512]{1,0:T(8,128)(2,1)} async-done(((bf16[768,512]{1,0:T(8,128)(2,1)}), bf16[384,512]{1,0:T(8,128)(2,1)}) %reduce-scatter.7.cloned.1.call-update) | async-done | bytes 393232
  275.3 1.2 copy.48
  276.8 2.6 collective-permute-start
  280.6 0.7 fusion.16
  283.3 2.2 collective-permute-start.2
  285.5 0.9 fusion.7
  286.8 3.3 collective-permute-start.1
  290.1 0.6 compare_reduce_fusion.4
  295.1 1.9 collective-permute-start.4
  297.5 3.1 collective-permute-start.3
  305.7 3.6 %collective-permute-done.4 = bf16[128,1536]{1,0:T(8,128)(2,1)S(1)} collective-permute-done((bf16[128,1536]{1,0:T(8,128)(2,1)S(1)}, bf16[128,1536]{1,0:T(8,128)(2,1)S(1)}, u32[]{:S(2)}, u32[]{:S(2)}) %collective-permute-start.4) | collective-permute-done | bytes 393248 | tf_op jit(solution)/shard_map/ppermute | solution.py:17
  309.6 5.5 %collective-permute-start.5 = (bf16[128,128]{0,1:T(8,128)(2,1)S(1)}, bf16[128,128]{0,1:T(8,128)(2,1)S(1)}, u32[]{:S(2)}, u32[]{:S(2)}) collective-permute-start(bf16[128,128]{0,1:T(8,128)(2,1)S(1)} %get-tuple-element.16), channel_id=1, source_target_pairs={{0,24},{8,32},{16,40},{24,48},{32,56},{40,64},{48,72},{56,80},{64,... | collective-permute-start | bytes 98312 | tf_op jit(solution)/shard_map/ppermute | solution.py:17
  315.1 0.6 compare_reduce_fusion
  317.8 0.8 slice.7
  318.7 3.9 %all-to-all-start = ((bf16[8,128,256]{1,2,0:T(8,128)(2,1)}), bf16[8,128,256]{1,2,0:T(8,128)(2,1)S(1)}, u32[]{:S(2)}, u32[]{:S(2)}) async-start(bf16[8,128,256]{1,2,0:T(8,128)(2,1)} %bitcast.20), calls=%async_computation.1 | async-start | bytes 1048576 | tf_op jit(solution)/shard_map/all_to_all | solution.py:33
  322.6 0.8 reshape.31
  323.5 7.9 %all-to-all-done = bf16[8,128,256]{1,2,0:T(8,128)(2,1)S(1)} async-done(((bf16[8,128,256]{1,2,0:T(8,128)(2,1)}), bf16[8,128,256]{1,2,0:T(8,128)(2,1)S(1)}, u32[]{:S(2)}, u32[]{:S(2)}) %all-to-all-start) | async-done | bytes 524320 | tf_op jit(solution)/shard_map/all_to_all | solution.py:33
  331.4 0.8 copy.32
  (41 shorter events, 5.1 us)
Async XLA Ops:
  7.2 3.9 %copy-start = (f32[8,8,2,2]{1,3,2,0:T(2,128)S(1)}, f32[8,8,2,2]{1,3,2,0:T(2,128)}, u32[]{:S(2)}) copy-start(f32[8,8,2,2]{1,3,2,0:T(2,128)} %param.8) | copy-start | bytes 3076
  7.2 62.2 %all-gather.3.cloned.1.call-start = ((), (), s32[]{:S(2)}) async-start(), calls=%async_computation.3 | async-start | bytes 10027008 | tf_op jit(solution)/shard_map/all_gather | solution.py:66
  7.9 165.5 %all-gather.5.cloned.1.call-start = ((), (), s32[]{:S(2)}) async-start(), calls=%async_computation.4 | async-start | bytes 20054016 | tf_op jit(solution)/shard_map/all_gather | solution.py:75
  11.0 240.6 %reduce-scatter.5.cloned.1.call-start = ((), (), s32[]{:S(2)}) async-start(), calls=%async_computation.5 | async-start | bytes 3932160 | tf_op jit(solution)/shard_map/reduce_scatter | solution.py:22
  84.9 15.2 %copy-start.2 = (f32[8,8,2,2,2,2]{1,0,5,4,3,2:T(8,128)S(1)}, f32[8,8,2,2,2,2]{1,0,5,4,3,2:T(8,128)}, u32[]{:S(2)}) copy-start(f32[8,8,2,2,2,2]{1,0,5,4,3,2:T(8,128)} %copy.25) | copy-start | bytes 12292
  212.5 68.1 %copy-start.3 = (s32[16]{0:T(128)S(1)}, s32[16]{0:T(128)}, u32[]{:S(2)}) copy-start(s32[16]{0:T(128)} %param.11) | copy-start | bytes 196
  212.5 119.6 %copy-start.1 = (f32[8,8,2,2]{1,3,2,0:T(2,128)S(1)}, f32[8,8,2,2]{1,3,2,0:T(2,128)}, u32[]{:S(2)}) copy-start(f32[8,8,2,2]{1,3,2,0:T(2,128)} %param.8) | copy-start | bytes 3076
  212.5 62.8 %reduce-scatter.7.cloned.1.call-start = ((), (), s32[]{:S(2)}) async-start(), calls=%async_computation.6 | async-start | bytes 1179648
  276.8 9.7 %collective-permute-start = (bf16[128,1536]{1,0:T(8,128)(2,1)S(1)}, bf16[128,1536]{1,0:T(8,128)(2,1)S(1)}, u32[]{:S(2)}, u32[]{:S(2)}) collective-permute-start(bf16[128,1536]{1,0:T(8,128)(2,1)S(1)} %reshape_reshape.3), channel_id=1, source_target_pairs={{8,0},{16,8},{24,16},{32,24},{40,32},{48,40},{56,48},{64,56},{72,6... | collective-permute-start | bytes 1179656 | tf_op jit(solution)/shard_map/ppermute | solution.py:17
  283.3 14.0 %collective-permute-start.2 = (bf16[128,1536]{1,0:T(8,128)(2,1)S(1)}, bf16[128,1536]{1,0:T(8,128)(2,1)S(1)}, u32[]{:S(2)}, u32[]{:S(2)}) collective-permute-start(bf16[128,1536]{1,0:T(8,128)(2,1)S(1)} %reshape_reshape.3), channel_id=1, source_target_pairs={{16,0},{24,8},{32,16},{40,24},{48,32},{56,40},{64,48},{72,56},{80,... | collective-permute-start | bytes 1179656 | tf_op jit(solution)/shard_map/ppermute | solution.py:17
  286.8 10.3 %collective-permute-start.1 = (bf16[128,128]{0,1:T(8,128)(2,1)S(1)}, bf16[128,128]{0,1:T(8,128)(2,1)S(1)}, u32[]{:S(2)}, u32[]{:S(2)}) collective-permute-start(bf16[128,128]{0,1:T(8,128)(2,1)S(1)} %get-tuple-element.12), channel_id=1, source_target_pairs={{0,8},{8,16},{16,24},{24,32},{32,40},{40,48},{48,56},{56,64},{64,7... | collective-permute-start | bytes 98312 | tf_op jit(solution)/shard_map/ppermute | solution.py:17
  295.1 14.2 %collective-permute-start.4 = (bf16[128,1536]{1,0:T(8,128)(2,1)S(1)}, bf16[128,1536]{1,0:T(8,128)(2,1)S(1)}, u32[]{:S(2)}, u32[]{:S(2)}) collective-permute-start(bf16[128,1536]{1,0:T(8,128)(2,1)S(1)} %reshape_reshape.3), channel_id=1, source_target_pairs={{24,0},{32,8},{40,16},{48,24},{56,32},{64,40},{72,48},{80,56},{88,... | collective-permute-start | bytes 1179656 | tf_op jit(solution)/shard_map/ppermute | solution.py:17
  297.5 8.0 %collective-permute-start.3 = (bf16[128,128]{0,1:T(8,128)(2,1)S(1)}, bf16[128,128]{0,1:T(8,128)(2,1)S(1)}, u32[]{:S(2)}, u32[]{:S(2)}) collective-permute-start(bf16[128,128]{0,1:T(8,128)(2,1)S(1)} %get-tuple-element.14), channel_id=1, source_target_pairs={{0,16},{8,24},{16,32},{24,40},{32,48},{40,56},{48,64},{56,72},{64,... | collective-permute-start | bytes 98312 | tf_op jit(solution)/shard_map/ppermute | solution.py:17
  309.6 8.1 %collective-permute-start.5 = (bf16[128,128]{0,1:T(8,128)(2,1)S(1)}, bf16[128,128]{0,1:T(8,128)(2,1)S(1)}, u32[]{:S(2)}, u32[]{:S(2)}) collective-permute-start(bf16[128,128]{0,1:T(8,128)(2,1)S(1)} %get-tuple-element.16), channel_id=1, source_target_pairs={{0,24},{8,32},{16,40},{24,48},{32,56},{40,64},{48,72},{56,80},{64,... | collective-permute-start | bytes 98312 | tf_op jit(solution)/shard_map/ppermute | solution.py:17
  318.7 12.6 %all-to-all-start = ((bf16[8,128,256]{1,2,0:T(8,128)(2,1)}), bf16[8,128,256]{1,2,0:T(8,128)(2,1)S(1)}, u32[]{:S(2)}, u32[]{:S(2)}) async-start(bf16[8,128,256]{1,2,0:T(8,128)(2,1)} %bitcast.20), calls=%async_computation.1 | async-start | bytes 1048576 | tf_op jit(solution)/shard_map/all_to_all | solution.py:33
Sparse Core Ops, SparseCore 0:
  9.7 59.6 all-gather.2
  71.1 102.2 all-gather.4
  212.7 38.8 reduce-scatter.4
  254.0 21.3 reduce-scatter.6
where the time goes:
time: 342 us; the launch traced here: 339 us
  waiting for transfers between devices  196 us (57%)
  local copies, waits for them, and re-layouts  50.6 us (15%)
  matrix products  38.8 us (11%)
  between operations  25.3 us (7%)
  starting transfers between devices  22.7 us (7%)
  other arithmetic  5.29 us (2%)
    all_gather x1, waiting for transfers between devices, shards(): columns_piece = lax.all_gather(right_environment, 'lb', axis=2, tiled=True)  66.9 us
    all_gather x1, waiting for transfers between devices, shards(): rows_piece = lax.all_gather(wavefunction, 'lb', axis=0, tiled=True)  56.5 us
    reduce_scatter x1, waiting for transfers between devices, summed_rows(): value = lax.psum_scatter(value, axis, scatter_dimension=dim, tiled=True)  38.9 us
    all_gather x1, local copies, waits for them, and re-layouts, shards(): columns_piece = lax.all_gather(right_environment, 'lb', axis=2, tiled=True)  24 us
    unnamed x5, waiting for transfers between devices  22.2 us
    ppermute x6, starting transfers between devices, shifted(): return lax.ppermute(value, axis, pairs)  18.5 us
    reshape x1, local copies, waits for them, and re-layouts, shards(): flat_piece = rows_piece.reshape(rows_piece.shape[0], 4 * local_right)  15.5 us
    dot_general x1, matrix products, shards(): jnp.dot(left_matrix, flat_piece, preferred_element_type=jnp.float32)  15.2 us
  transfers between devices with their start and end apart: 11, of which 6 were waited for; matrix products, arithmetic and copies ran while one was open for 15% of the time, Pallas kernels for 0%

commit v1 on v0

v1 whole, which is shorter than its diff:
```python
import functools
import math

import jax
import jax.numpy as jnp
from jax import lax
from jax.experimental import pallas as pl
from jax.experimental.pallas import tpu as pltpu
from jax.sharding import Mesh
from jax.sharding import PartitionSpec as P

BOND_WIDTH = 3072
SECTOR_TILES = 4
AXES = ("zl", "y", "core", "x", "zh")
LB = ("zl", "y", "core")
RB = ("x", "zh")
BF16, F32 = jnp.bfloat16, jnp.float32

MAIN, REST = 128, 64
PIECES = (
    (("z", 1, 0, 64), ("z", -1, 64, 48), ("y", 1, 112, 32), ("y", -1, 144, 48)),
    (("z", 1, 0, 32), ("z", -1, 32, 32), ("y", 1, 64, 32), ("y", -1, 96, 32)),
    (("z", 1, 0, 32), ("z", -1, 32, 16), ("y", -1, 48, 16)),
)
UNIT_BYTES = (1536 * 2, 8 * 384 * 2, 8 * 384 * 2)
SHARD = (192, MAIN, REST)
SOURCES = tuple((dz, dy) for dz in (0, 1) for dy in range(4))
MESSAGES = tuple(
    (phase, piece, source)
    for phase in range(3)
    for piece in range(len(PIECES[phase]))
    for source in SOURCES[1:]
)


def forwards(phase, piece, source):
    tree, turn = PIECES[phase][piece][:2]
    (dz, dy), on, back = source, "+-"[turn < 0], (-turn) % 4
    named = lambda link, place: (link, (phase, piece, place))
    if tree == "z":
        if source == (1, 0):
            return [named("+", (1, 3)), named("-", (1, 1))]
        return [named(on, (dz, 2))] if dy == back else []
    if dz:
        return []
    across = [named("z", (1, dy))]
    return [named(on, (0, 2)), *across] if dy == back else across


def own_sends():
    for phase in range(3):
        pieces = range(len(PIECES[phase]))
        for piece in sorted(pieces, key=lambda p: PIECES[phase][p][0] == "y"):
            yield "z", (phase, piece, (1, 0))
        for piece in sorted(pieces, key=lambda p: PIECES[phase][p][0] == "z"):
            yield "+", (phase, piece, (0, 3))
            yield "-", (phase, piece, (0, 1))


def schedule(rate=43.5e3, lag=1.0, lead=5.0, step=0.05):
    spent = {"first": 3.0, "mix": 1.6, "second": (None, 1.6, 1.3)}
    waiting = {link: [] for link in "+-z"}
    for order, (link, message) in enumerate(own_sends()):
        waiting[link].append((message[0], order, message, True))
    free_at = dict.fromkeys("+-z", 0.0)
    arriving, beside, done, ops, issued = [], [], set(), [], []
    pieces_left = {(p, s): len(PIECES[p]) for p in range(3) for s in SOURCES[1:]}
    ready = {(p, s): None for p in range(3) for s in SOURCES}
    for phase in range(3):
        ready[phase, (0, 0)] = 4.0 + phase
    firsts, mixes, seconds = 0, 0, [0, 0]
    order, now, tc_free = 1000, 0.0, 0.0
    while seconds[1] < 8:
        now += step
        for link in "+-z":
            if free_at[link] <= now and waiting[link]:
                job = min(waiting[link])
                waiting[link].remove(job)
                phase, piece, _ = message = job[2]
                took = PIECES[phase][piece][3] * UNIT_BYTES[phase] / rate
                if job[3]:
                    issued.append((max(0.0, now - lead), len(issued), link, message))
                free_at[link] = now + took
                arriving.append((now + took + lag, message))
        if tc_free > now:
            continue
        landed = [entry for entry in arriving if entry[0] <= now]
        if landed:
            entry = min(landed)
            arriving.remove(entry)
            message = entry[1]
            onward = forwards(*message)
            for link, passed in onward:
                order += 1
                waiting[link].append((passed[0], order, passed, False))
            ops.append((now, "take", message, onward))
            phase, _, source = message
            pieces_left[phase, source] -= 1
            if not pieces_left[phase, source]:
                ops.append((now, "share", phase, source))
                size = SHARD[phase] * UNIT_BYTES[phase]
                ready[phase, source] = now + 2.0 + size / 400e3
            tc_free = now + 0.2
            continue
        able = [k for k, at in ready.items() if at is not None and at <= now and k not in done]
        able = [k for k in able if k[0] == 0 or mixes == 4]
        if firsts == 8 and mixes < 4:
            ops.append((now, "mix", mixes))
            mixes += 1
            tc_free = now + spent["mix"]
        elif able:
            phase, source = min(able, key=lambda k: (k[0], ready[k]))
            done.add((phase, source))
            if phase == 0:
                ops.append((now, "first", source, firsts == 0))
                firsts += 1
                tc_free = now + spent["first"]
            else:
                ops.append((now, "second", phase, source))
                seconds[phase - 1] += 1
                tc_free = now + spent["second"][phase]
                if seconds[phase - 1] == 8:
                    ops.append((tc_free, "sum", phase))
    for at, _, link, message in reversed(issued):
        place = next((i for i, op in enumerate(ops) if op[0] > at), len(ops))
        ops.insert(place, (at, "send", link, message))
    return [op[1:] for op in ops], now


def ring(value, by, size):
    return lax.rem(value + (by % size), size)


def kernel(
    ops, w_ref, l_ref, r_ref, comb_ref, out_ref,
    left, wide, main, rest, acc, mixed, coef, part_main, part_rest, from_main, from_rest,
    kept_main, kept_rest, away_main, away_rest, back_main, back_rest,
    local_sem, send_sem, recv_sem, share_send, share_recv, x_send, x_recv, z_send, z_recv,
):
    zl, y, core, x, zh = (lax.axis_index(a) for a in AXES)
    gathered = (wide, main, rest)
    number = {m: i for i, m in enumerate(MESSAGES)}
    neighbour = {
        "+": {"y": ring(y, 1, 4)},
        "-": {"y": ring(y, -1, 4)},
        "z": {"zl": 1 - zl},
    }
    mesh_type = pl.DeviceIdType.MESH

    def chip(source):
        dz, dy = source
        return (1 - zl if dz else zl) * 4 + ring(y, dy, 4)

    barrier = pltpu.get_barrier_semaphore()
    partners = [*neighbour.values(), {"core": 1 - core}, {"zh": 1 - zh}]
    partners += [{"x": ring(x, by, 4)} for by in (1, 2, 3)]
    for partner in partners:
        pl.semaphore_signal(barrier, inc=1, device_id=partner, device_id_type=mesh_type)

    here = chip((0, 0)) * 2 + core
    loads = [
        pltpu.make_async_copy(w_ref, wide.at[here], local_sem.at[0]),
        pltpu.make_async_copy(r_ref.at[:, 0:MAIN], main.at[here], local_sem.at[1]),
        pltpu.make_async_copy(r_ref.at[:, MAIN : MAIN + REST], rest.at[here], local_sem.at[2]),
        pltpu.make_async_copy(l_ref, left, local_sem.at[3]),
    ]
    for load in loads:
        load.start()
    row = lax.broadcasted_iota(jnp.int32, (256, 32), 0)
    column = lax.broadcasted_iota(jnp.int32, (256, 32), 1)
    spread = (row // 8 == column).astype(BF16)
    row = lax.broadcasted_iota(jnp.int32, (256, 256), 0)
    column = lax.broadcasted_iota(jnp.int32, (256, 256), 1)
    same = row % 8 == column % 8
    high = comb_ref[...].astype(BF16)
    low = (comb_ref[...] - high.astype(F32)).astype(BF16)
    for at, term in enumerate((high, low)):
        tall = jnp.dot(spread, term, preferred_element_type=F32).astype(BF16)
        full = lax.dot_general(tall, spread, (((1,), (1,)), ((), ())), preferred_element_type=F32)
        coef[at * 256 : at * 256 + 256] = jnp.where(same, full, 0.0).astype(BF16)
    pl.semaphore_wait(barrier, len(partners))
    for load in loads:
        load.wait()

    sent = []

    def piece_of(message, receiver):
        phase, piece, _ = message
        start, size = PIECES[phase][piece][2:]
        if phase == 0:
            return wide.at[receiver, pl.ds(start, size)]
        return gathered[phase].at[receiver, :, pl.ds(start, size)]

    def send(link, message, source):
        block = piece_of(message, chip(source) * 2 + core)
        at = number[message]
        copy = pltpu.make_async_remote_copy(
            block, block, send_sem.at[at], recv_sem.at[at],
            device_id=neighbour[link], device_id_type=mesh_type,
        )
        copy.start()
        sent.append(copy)

    def arrived(message):
        block = piece_of(message, chip(message[2]) * 2 + core)
        at = number[message]
        pltpu.make_async_remote_copy(
            block, block, send_sem.at[at], recv_sem.at[at],
            device_id=neighbour["z"], device_id_type=mesh_type,
        ).wait_recv()

    def share(phase, source, owner):
        at = phase * 8 + SOURCES.index(source)
        block = gathered[phase].at[chip(source) * 2 + owner]
        return pltpu.make_async_remote_copy(
            block, block, share_send.at[at], share_recv.at[at],
            device_id={"core": 1 - core}, device_id_type=mesh_type,
        )

    def first(source, fresh):
        k = chip(source)
        columns = pl.ds(pl.multiple_of(k * 384, 384), 384)

        @pl.loop(0, 6)
        def _(tile):
            lanes = pl.ds(pl.multiple_of(tile * 256, 256), 256)
            block = wide[pl.ds(k * 2, 2), :, lanes].reshape(384, 256)
            product = jnp.dot(left[:, columns], block, preferred_element_type=F32)
            if fresh:
                acc[:, lanes] = product
            else:
                acc[:, lanes] += product

    def mix(quarter):
        @pl.loop(quarter * 2, quarter * 2 + 2)
        def _(group):
            halves = []
            for sub in range(2):
                start = pl.multiple_of(group * 16 + sub * 8, 8)
                stack = jnp.concatenate(
                    [
                        acc[pl.ds(a * 128 + start, 8), s * 384 : s * 384 + 384]
                        for a in range(8)
                        for s in range(4)
                    ],
                    axis=0,
                )
                top = stack.astype(BF16)
                under = (stack - top.astype(F32)).astype(BF16)
                both = jnp.dot(coef[...], top, preferred_element_type=F32)
                third = jnp.dot(coef[0:256], under, preferred_element_type=F32)
                halves.append(both[0:256] + both[256:512] + third)
            for v in range(8):
                for out_site in range(4):
                    at = (v * 4 + out_site) * 8
                    value = jnp.concatenate([h[at : at + 8] for h in halves], axis=0)
                    rows = pl.ds(pl.multiple_of(out_site * 128 + group * 16, 16), 16)
                    mixed[rows, v * 384 : v * 384 + 384] = value.astype(BF16)

    parts, froms = (None, part_main, part_rest), (None, from_main, from_rest)
    keeps, aways, backs = (None, kept_main, kept_rest), (None, away_main, away_rest), (None, back_main, back_rest)

    def to_owner(phase, k):
        owner, half = k // 2, lax.rem(k, 2)
        slot = lax.rem(x - owner + 7, 4)
        slot = jnp.minimum(slot, 2)
        copy = pltpu.make_async_remote_copy(
            parts[phase].at[k], froms[phase].at[half, slot],
            x_send.at[(phase - 1) * 8 + k], x_recv.at[(phase - 1) * 6 + half * 3 + slot],
            device_id={"x": owner}, device_id_type=mesh_type,
        )
        return copy, x != owner

    def second(phase, source):
        k = chip(source)
        width = 2 * SHARD[phase]

        @pl.loop(0, 4)
        def _(tile):
            rows = pl.ds(pl.multiple_of(tile * 128, 128), 128)
            total = None
            for v in range(8):
                block = gathered[phase][pl.ds(k * 2, 2), v].reshape(width, 384)
                product = lax.dot_general(
                    mixed[rows, v * 384 : v * 384 + 384], block,
                    (((1,), (1,)), ((), ())), preferred_element_type=F32,
                )
                total = product if total is None else total + product
            parts[phase][k, rows] = total.astype(BF16)

        copy, away = to_owner(phase, k)

        @pl.when(away)
        def _():
            copy.start()

    def z_copy(phase):
        return pltpu.make_async_remote_copy(
            aways[phase], backs[phase], z_send.at[phase - 1], z_recv.at[phase - 1],
            device_id={"zh": 1 - zh}, device_id_type=mesh_type,
        )

    def sum_x(phase, half, put):
        for slot in range(3):
            pltpu.make_async_remote_copy(
                parts[phase].at[0], froms[phase].at[half, slot],
                x_send.at[0], x_recv.at[(phase - 1) * 6 + half * 3 + slot],
                device_id={"x": ring(x, 1, 4)}, device_id_type=mesh_type,
            ).wait_recv()

        @pl.loop(0, 8)
        def _(tile):
            rows = pl.ds(pl.multiple_of(tile * 64, 64), 64)
            total = parts[phase][x * 2 + half, rows].astype(F32)
            for slot in range(3):
                total += froms[phase][half, slot, rows].astype(F32)
            put(rows, total)

    def sum_parts(phase):
        def put_away(rows, total):
            aways[phase][rows] = total.astype(BF16)

        def put_kept(rows, total):
            keeps[phase][rows] = total

        sum_x(phase, 1 - zh, put_away)
        z_copy(phase).start()
        sum_x(phase, zh, put_kept)

    def finish(phase):
        z_copy(phase).wait_recv()
        start, width = (0, 2 * MAIN) if phase == 1 else (2 * MAIN, 2 * REST)
        for site in range(4):
            rows = slice(site * 128, site * 128 + 128)
            value = keeps[phase][rows] + backs[phase][rows].astype(F32)
            out_ref[site, :, start : start + width] = value.astype(BF16)

    for phase in range(3):
        share(phase, (0, 0), core).start()
    for op in ops:
        if op[0] == "send":
            send(op[1], op[2], (0, 0))
        elif op[0] == "take":
            arrived(op[1])
            for link, passed in op[2]:
                send(link, passed, op[1][2])
        elif op[0] == "share":
            share(op[1], op[2], core).start()
        elif op[0] == "first":
            share(0, op[1], 1 - core).wait_recv()
            first(op[1], op[2])
        elif op[0] == "mix":
            mix(op[1])
        elif op[0] == "second":
            share(op[1], op[2], 1 - core).wait_recv()
            second(op[1], op[2])
        elif op[0] == "sum":
            sum_parts(op[1])
    for phase in (1, 2):
        finish(phase)
    for copy in sent:
        copy.wait_send()
    for phase in range(3):
        for source in SOURCES:
            share(phase, source, core).wait_send()
    for phase in (1, 2):
        z_copy(phase).wait_send()
        for k in range(8):
            copy, away = to_owner(phase, k)

            @pl.when(away)
            def _(copy=copy):
                copy.wait_send()


def applied_of(wavefunction, left_environment, combined, right_environment):
    ops, _ = schedule()
    vmem = pltpu.VMEM
    dma = pltpu.SemaphoreType.DMA
    count = len(MESSAGES)
    scratch = [
        vmem((1024, 3072), BF16), vmem((16, 192, 1536), BF16), vmem((16, 8, MAIN, 384), BF16),
        vmem((16, 8, REST, 384), BF16), vmem((1024, 1536), F32), vmem((512, 3072), BF16),
        vmem((512, 256), BF16), vmem((8, 512, 256), BF16), vmem((8, 512, 128), BF16),
        vmem((2, 3, 512, 256), BF16), vmem((2, 3, 512, 128), BF16),
        vmem((512, 256), F32), vmem((512, 128), F32), vmem((512, 256), BF16), vmem((512, 128), BF16),
        vmem((512, 256), BF16), vmem((512, 128), BF16),
        dma((4,)), dma((count,)), dma((count,)), dma((24,)), dma((24,)), dma((16,)), dma((12,)),
        dma((2,)), dma((2,)),
    ]
    spec = pl.BlockSpec(memory_space=pl.ANY)
    return pl.pallas_call(
        functools.partial(kernel, ops),
        out_shape=jax.ShapeDtypeStruct((4, 128, 384), BF16),
        in_specs=[spec, spec, spec, pl.BlockSpec(memory_space=pltpu.VMEM)],
        out_specs=pl.BlockSpec(memory_space=pltpu.VMEM),
        scratch_shapes=scratch,
        compiler_params=pltpu.CompilerParams(
            collective_id=0, has_side_effects=True, vmem_limit_bytes=61 << 20
        ),
    )(
        wavefunction.reshape(192, 1536),
        left_environment.reshape(1024, 3072),
        right_environment.transpose(0, 2, 1),
        combined,
    )


def combine_operators(operator_left, operator_right):
    channels = operator_left.shape[0]
    joined = jnp.einsum(
        "aups,uvqt->vpqast", operator_left, operator_right, precision=lax.Precision.HIGHEST
    )
    return joined.reshape(4 * channels, 4 * channels)


def split_up(value, dim, devices):
    before, after = (value.shape[:dim], value.shape[dim + 1 :])
    return jnp.moveaxis(value.reshape(*before, devices, -1, *after), dim, 0)


def sent_and_summed(value, axis, dim):
    parts = split_up(value, dim, lax.axis_size(axis))
    arrived = lax.all_to_all(parts, axis, split_axis=0, concat_axis=0, tiled=True)
    return arrived.astype(jnp.float32).sum(axis=0)


def shifted(value, axis, by):
    devices = lax.axis_size(axis)
    pairs = [(i, i + by) for i in range(devices) if 0 <= i + by < devices]
    return lax.ppermute(value, axis, pairs)


def label_at(labels, position):
    matches = jnp.arange(labels.shape[0], dtype=jnp.int32) == position
    return (jnp.sum(jnp.where(matches, labels, 0)), jnp.any(matches))


def tile_gram(left_tile, right_tile):
    return lax.dot_general(
        left_tile, right_tile, (((1,), (1,)), ((), ())), preferred_element_type=jnp.float32
    )


def shards(
    wavefunction, left_environment, operator_left, operator_right, right_environment, row_sector
):
    combined = combine_operators(operator_left, operator_right)
    raw = applied_of(wavefunction, left_environment, combined, right_environment)
    raw = raw.transpose(1, 0, 2)
    applied = jnp.concatenate(
        [raw[..., 0:128], raw[..., 256:320], raw[..., 128:256], raw[..., 320:384]], axis=2
    )
    row_count = 128
    own_tile = applied.reshape(row_count, 4 * 384)
    own_index = lax.axis_index(LB)
    tile_count = 16
    reach_tiles = SECTOR_TILES - 1
    own_label = label_at(row_sector, own_index)[0]
    buffer = jnp.zeros((row_count, (tile_count + 2 * reach_tiles) * row_count), jnp.float32)

    def place_block(buffer, gram_block, offset):
        mate_index = own_index + offset
        mate_label, inside = label_at(row_sector, mate_index)
        keep_block = jnp.logical_and(inside, mate_label == own_label)
        gram_block = jnp.where(keep_block, gram_block, jnp.float32(0.0))
        column_start = (mate_index + reach_tiles) * row_count
        return lax.dynamic_update_slice(buffer, gram_block, (jnp.int32(0), column_start))

    buffer = place_block(buffer, tile_gram(own_tile, own_tile), 0)
    for distance in range(1, SECTOR_TILES):
        gram_block = tile_gram(own_tile, shifted(own_tile, LB, -distance))
        buffer = place_block(buffer, gram_block, distance)
        returned = shifted(gram_block.astype(jnp.bfloat16), LB, distance).astype(gram_block.dtype)
        buffer = place_block(buffer, returned.T, -distance)
    full_rows = buffer[:, reach_tiles * row_count : (reach_tiles + tile_count) * row_count]
    density = sent_and_summed(full_rows.astype(jnp.bfloat16), RB, 1) * (
        1.0 / math.sqrt(4.0 * BOND_WIDTH)
    )
    return (applied, density)


def solution(mesh):
    torus = Mesh(mesh.devices.reshape(2, 4, 2, 4, 2), AXES)
    in_specs = (P(LB, None, RB), P(None, LB, None), P(), P(), P(None, RB, LB), P())
    out_specs = (P(LB, None, RB), P(LB, RB))
    return jax.shard_map(
        shards, mesh=torus, in_specs=in_specs, out_specs=out_specs, check_vma=False
    )
```

time: 342 us -> 208 us (0.61)
  waiting for transfers between devices: 196 us -> 12.6 us
  Pallas kernels: 0 us -> 138 us
  local copies, waits for them, and re-layouts: 50.6 us -> 8.82 us
  matrix products: 38.8 us -> 3.07 us
  between operations: 25.3 us -> 12.1 us
    pallas_call x0 -> x1, Pallas kernels: none -> 138 us  [applied_of(): pl.pallas_call(functools.partial(kernel, ops), out_shape=jax.ShapeDtypeSt...]
    all_gather x2 -> x0, waiting for transfers between devices: 123 us -> none  [the longest x1 66.9 us: shards(): columns_piece = lax.all_gather(right_environment, 'lb', axis=2, tiled=True)]
    reduce_scatter x1 -> x0, waiting for transfers between devices: 38.9 us -> none  [summed_rows(): value = lax.psum_scatter(value, axis, scatter_dimension=dim, tiled=True)]
    dot_general x4 -> x1, matrix products: 37.1 us -> 1.13 us  [combine_operators(): jnp.einsum('aups,uvqt->vpqast', operator_left, operator_right, precision=...]
    all_gather x1 -> x0, local copies, waits for them, and re-layouts: 24 us -> none  [shards(): columns_piece = lax.all_gather(right_environment, 'lb', axis=2, tiled=True)]
    unnamed x5 -> x0, waiting for transfers between devices: 22.2 us -> none
    reshape x2 -> x1, local copies, waits for them, and re-layouts: 16.4 us -> 0.96 us  [combine_operators(): return joined.reshape(4 * channels, 4 * channels)]
    unnamed x13 -> x7, local copies, waits for them, and re-layouts: 7.98 us -> 3.77 us
  transfers between devices with their start and end apart: 11 -> 7, of which waited for: 6 -> 2; matrix products, arithmetic and copies ran while one was open for 15% -> 4% of each run, Pallas kernels for 0% -> 0%
where the time goes in v1:
time: 208 us; the launch traced here: 206 us
  Pallas kernels  138 us (66%)
  starting transfers between devices  25.6 us (12%)
  waiting for transfers between devices  12.6 us (6%)
  between operations  12.1 us (6%)
  local copies, waits for them, and re-layouts  8.82 us (4%)
  other arithmetic  5.5 us (3%)
  matrix products  3.07 us (1%)
    pallas_call x1, Pallas kernels, applied_of(): pl.pallas_call(functools.partial(kernel, ops), out_shape=jax.ShapeDtypeSt...  138 us
    ppermute x6, starting transfers between devices, shifted(): return lax.ppermute(value, axis, pairs)  18.5 us
    all_to_all x1, waiting for transfers between devices, sent_and_summed(): lax.all_to_all(parts, axis, split_axis=0, concat_axis=0, tiled=True)  9.07 us
    all_to_all x1, starting transfers between devices, sent_and_summed(): lax.all_to_all(parts, axis, split_axis=0, concat_axis=0, tiled=True)  7.03 us
    reduce_or x7, other arithmetic, label_at(): return (jnp.sum(jnp.where(matches, labels, 0)), jnp.any(matches))  4.44 us
  transfers between devices with their start and end apart: 7, of which 2 were waited for; matrix products, arithmetic and copies ran while one was open for 4% of the time, Pallas kernels for 0%

profile of v1, /device:TPU:9, one launch (start us, length us, event | category | flops | bytes accessed | tf_op | source)
XLA Modules:
  0.0 205.7 jit_solution(2636196334224146531)
XLA Ops:
  0.6 2.0 copy.38
  2.6 1.1 convolution_bitcast_fusion.1
  3.7 0.5 copy.25
  4.2 1.0 reshape.21.comb_ref
  5.2 138.1 %shard_map.77 = bf16[4,128,384]{2,1,0:T(8,128)(2,1)} custom-call(bf16[192,1536]{1,0:T(8,128)(2,1)} %bitcast.41, bf16[1024,3072]{1,0:T(8,128)(2,1)} %bitcast.34, bf16[8,192,384]{2,1,0:T(8,128)(2,1)} %bitcast.44, f32[32,32]{1,0:T(8,128)} %reshape.21.comb_ref), custom_call_target="tpu_custom_call" | custom-call | tf_op jit(solution)/shard_map/pallas_call | solution.py:392
  143.3 1.0 fusion.11
  144.3 1.1 fusion.12
  145.6 0.2 copy.26
  145.8 1.9 collective-permute-start
  147.7 1.9 collective-permute-start.2
  149.7 0.6 compare_reduce_fusion.6
  150.3 0.6 compare_reduce_fusion.5
  150.9 0.7 fusion.10
  153.7 0.9 fusion.1
  154.6 3.5 %collective-permute-done = bf16[128,1536]{0,1:T(8,128)(2,1)S(1)} collective-permute-done((bf16[128,1536]{0,1:T(8,128)(2,1)S(1)}, bf16[128,1536]{0,1:T(8,128)(2,1)S(1)}, u32[]{:S(2)}, u32[]{:S(2)}) %collective-permute-start) | collective-permute-done | bytes 393248 | tf_op jit(solution)/shard_map/ppermute | solution.py:431
  158.1 0.3 select_dynamic-update-slice_fusion.2
  158.4 1.9 collective-permute-start.1
  160.4 1.9 collective-permute-start.4
  162.3 0.6 compare_reduce_fusion.4
  162.9 0.6 compare_reduce_fusion.3
  167.5 0.3 select_dynamic-update-slice_fusion.1
  167.9 3.8 %collective-permute-start.3 = (bf16[128,128]{0,1:T(8,128)(2,1)S(1)}, bf16[128,128]{0,1:T(8,128)(2,1)S(1)}, u32[]{:S(2)}, u32[]{:S(2)}) collective-permute-start(bf16[128,128]{0,1:T(8,128)(2,1)S(1)} %get-tuple-element.22), channel_id=1, source_target_pairs={{0,16},{8,24},{16,32},{24,40},{32,48},{40,56},{48,64},{56,72},{64,... | collective-permute-start | bytes 98312 | tf_op jit(solution)/shard_map/ppermute | solution.py:431
  171.6 0.6 compare_reduce_fusion.2
  172.3 0.6 compare_reduce_fusion.1
  176.7 0.3 select_dynamic-update-slice_fusion
  177.1 7.1 %collective-permute-start.5 = (bf16[128,128]{0,1:T(8,128)(2,1)S(1)}, bf16[128,128]{0,1:T(8,128)(2,1)S(1)}, u32[]{:S(2)}, u32[]{:S(2)}) collective-permute-start(bf16[128,128]{0,1:T(8,128)(2,1)S(1)} %get-tuple-element.24), channel_id=1, source_target_pairs={{0,24},{8,32},{16,40},{24,48},{32,56},{40,64},{48,72},{56,80},{64,... | collective-permute-start | bytes 98312 | tf_op jit(solution)/shard_map/ppermute | solution.py:431
  184.2 0.6 compare_reduce_fusion
  186.9 0.8 slice.27
  187.7 7.0 %all-to-all-start = ((bf16[8,128,256]{1,2,0:T(8,128)(2,1)}), bf16[8,128,256]{1,2,0:T(8,128)(2,1)S(1)}, u32[]{:S(2)}, u32[]{:S(2)}) async-start(bf16[8,128,256]{1,2,0:T(8,128)(2,1)} %bitcast.12), calls=%async_computation | async-start | bytes 1048576 | tf_op jit(solution)/shard_map/all_to_all | solution.py:424
  194.8 1.1 copy.30
  195.8 9.1 %all-to-all-done = bf16[8,128,256]{1,2,0:T(8,128)(2,1)S(1)} async-done(((bf16[8,128,256]{1,2,0:T(8,128)(2,1)}), bf16[8,128,256]{1,2,0:T(8,128)(2,1)S(1)}, u32[]{:S(2)}, u32[]{:S(2)}) %all-to-all-start) | async-done | bytes 524320 | tf_op jit(solution)/shard_map/all_to_all | solution.py:424
  205.0 0.8 copy.31
  (22 shorter events, 0.8 us)
Async XLA Ops:
  0.6 2.0 copy-start
  2.6 148.4 %copy-start.1 = (s32[16]{0:T(128)S(1)}, s32[16]{0:T(128)}, u32[]{:S(2)}) copy-start(s32[16]{0:T(128)} %param.11) | copy-start | bytes 196
  145.8 12.3 %collective-permute-start = (bf16[128,1536]{0,1:T(8,128)(2,1)S(1)}, bf16[128,1536]{0,1:T(8,128)(2,1)S(1)}, u32[]{:S(2)}, u32[]{:S(2)}) collective-permute-start(bf16[128,1536]{0,1:T(8,128)(2,1)S(1)} %bitcast.35), channel_id=1, source_target_pairs={{8,0},{16,8},{24,16},{32,24},{40,32},{48,40},{56,48},{64,56},{72,6... | collective-permute-start | bytes 1179656 | tf_op jit(solution)/shard_map/ppermute | solution.py:431
  147.7 19.8 %collective-permute-start.2 = (bf16[128,1536]{0,1:T(8,128)(2,1)S(1)}, bf16[128,1536]{0,1:T(8,128)(2,1)S(1)}, u32[]{:S(2)}, u32[]{:S(2)}) collective-permute-start(bf16[128,1536]{0,1:T(8,128)(2,1)S(1)} %bitcast.36), channel_id=1, source_target_pairs={{16,0},{24,8},{32,16},{40,24},{48,32},{56,40},{64,48},{72,56},{80,... | collective-permute-start | bytes 1179656 | tf_op jit(solution)/shard_map/ppermute | solution.py:431
  158.4 8.9 %collective-permute-start.1 = (bf16[128,128]{0,1:T(8,128)(2,1)S(1)}, bf16[128,128]{0,1:T(8,128)(2,1)S(1)}, u32[]{:S(2)}, u32[]{:S(2)}) collective-permute-start(bf16[128,128]{0,1:T(8,128)(2,1)S(1)} %get-tuple-element.20), channel_id=1, source_target_pairs={{0,8},{8,16},{16,24},{24,32},{32,40},{40,48},{48,56},{56,64},{64,7... | collective-permute-start | bytes 98312 | tf_op jit(solution)/shard_map/ppermute | solution.py:431
  160.4 16.3 %collective-permute-start.4 = (bf16[128,1536]{0,1:T(8,128)(2,1)S(1)}, bf16[128,1536]{0,1:T(8,128)(2,1)S(1)}, u32[]{:S(2)}, u32[]{:S(2)}) collective-permute-start(bf16[128,1536]{0,1:T(8,128)(2,1)S(1)} %bitcast.38), channel_id=1, source_target_pairs={{24,0},{32,8},{40,16},{48,24},{56,32},{64,40},{72,48},{80,56},{88,... | collective-permute-start | bytes 1179656 | tf_op jit(solution)/shard_map/ppermute | solution.py:431
  167.9 8.7 %collective-permute-start.3 = (bf16[128,128]{0,1:T(8,128)(2,1)S(1)}, bf16[128,128]{0,1:T(8,128)(2,1)S(1)}, u32[]{:S(2)}, u32[]{:S(2)}) collective-permute-start(bf16[128,128]{0,1:T(8,128)(2,1)S(1)} %get-tuple-element.22), channel_id=1, source_target_pairs={{0,16},{8,24},{16,32},{24,40},{32,48},{40,56},{48,64},{56,72},{64,... | collective-permute-start | bytes 98312 | tf_op jit(solution)/shard_map/ppermute | solution.py:431
  177.1 9.7 %collective-permute-start.5 = (bf16[128,128]{0,1:T(8,128)(2,1)S(1)}, bf16[128,128]{0,1:T(8,128)(2,1)S(1)}, u32[]{:S(2)}, u32[]{:S(2)}) collective-permute-start(bf16[128,128]{0,1:T(8,128)(2,1)S(1)} %get-tuple-element.24), channel_id=1, source_target_pairs={{0,24},{8,32},{16,40},{24,48},{32,56},{40,64},{48,72},{56,80},{64,... | collective-permute-start | bytes 98312 | tf_op jit(solution)/shard_map/ppermute | solution.py:431
  187.7 17.2 %all-to-all-start = ((bf16[8,128,256]{1,2,0:T(8,128)(2,1)}), bf16[8,128,256]{1,2,0:T(8,128)(2,1)S(1)}, u32[]{:S(2)}, u32[]{:S(2)}) async-start(bf16[8,128,256]{1,2,0:T(8,128)(2,1)} %bitcast.12), calls=%async_computation | async-start | bytes 1048576 | tf_op jit(solution)/shard_map/all_to_all | solution.py:424

commit v2 on v1

--- a/solution.py
+++ b/solution.py
@@ -33,6 +33,10 @@
 )
 
 
+FIRSTS = (((0, 0),), ((0, 1), (0, 3)), ((1, 0),), ((1, 1), (1, 3)), ((0, 2), (1, 2)))
+LATER = (("away", 10.0), ("keep", 1.0), ("finish", 6.0), ("swap", 0.5), ("gram", 9.0))
+
+
 def forwards(phase, piece, source):
     tree, turn = PIECES[phase][piece][:2]
     (dz, dy), on, back = source, "+-"[turn < 0], (-turn) % 4
@@ -58,7 +62,7 @@
 
 
 def schedule(rate=43.5e3, lag=1.0, lead=5.0, step=0.05):
-    spent = {"first": 3.0, "mix": 1.6, "second": (None, 1.6, 1.3)}
+    spent = (None, 1.1, 0.7)
     waiting = {link: [] for link in "+-z"}
     for order, (link, message) in enumerate(own_sends()):
         waiting[link].append((message[0], order, message, True))
@@ -69,6 +73,7 @@
     for phase in range(3):
         ready[phase, (0, 0)] = 4.0 + phase
     firsts, mixes, seconds = 0, 0, [0, 0]
+    later = []
     order, now, tc_free = 1000, 0.0, 0.0
     while seconds[1] < 8:
         now += step
@@ -103,39 +108,67 @@
             tc_free = now + 0.2
             continue
         able = [k for k, at in ready.items() if at is not None and at <= now and k not in done]
-        able = [k for k in able if k[0] == 0 or mixes == 4]
-        if firsts == 8 and mixes < 4:
+        group = FIRSTS[firsts] if firsts < len(FIRSTS) else None
+        due = [entry for entry in later if entry[0] <= now]
+        if group is not None:
+            if all((0, source) in able for source in group):
+                done.update((0, source) for source in group)
+                ops.append((now, "first", group, firsts == 0))
+                firsts += 1
+                tc_free = now + 1.0 + 1.1 * len(group)
+        elif mixes < 4:
             ops.append((now, "mix", mixes))
             mixes += 1
-            tc_free = now + spent["mix"]
+            tc_free = now + 1.1
+        elif due:
+            later.remove(due[0])
+            ops.append((now, *due[0][1:]))
+            tc_free = now + 0.7
         elif able:
             phase, source = min(able, key=lambda k: (k[0], ready[k]))
             done.add((phase, source))
-            if phase == 0:
-                ops.append((now, "first", source, firsts == 0))
-                firsts += 1
-                tc_free = now + spent["first"]
-            else:
-                ops.append((now, "second", phase, source))
-                seconds[phase - 1] += 1
-                tc_free = now + spent["second"][phase]
-                if seconds[phase - 1] == 8:
-                    ops.append((tc_free, "sum", phase))
+            ops.append((now, "second", phase, source))
+            seconds[phase - 1] += 1
+            tc_free = now + spent[phase]
+            if phase == 1 and seconds[0] == 8:
+                wait = 0.0
+                for name, gap in LATER:
+                    wait += gap
+                    later.append((tc_free + wait, name, 1))
+    ops += [(now, *entry[1:]) for entry in later]
+    ops += [(now, name, 2) for name, _ in LATER]
     for at, _, link, message in reversed(issued):
         place = next((i for i, op in enumerate(ops) if op[0] > at), len(ops))
         ops.insert(place, (at, "send", link, message))
     return [op[1:] for op in ops], now
 
 
+OFFSETS = (1, 2, 3, -1, -2, -3)
+
+
+def row_device(m):
+    return {"zl": m // 8, "y": lax.rem(m // 2, 4), "core": lax.rem(m, 2)}
+
+
+def column_device(n):
+    return {"x": n // 2, "zh": lax.rem(n, 2)}
+
+
+def inside(m):
+    return jnp.logical_and(m >= 0, m < 16)
+
+
 def ring(value, by, size):
     return lax.rem(value + (by % size), size)
 
 
 def kernel(
-    ops, w_ref, l_ref, r_ref, comb_ref, out_ref,
+    ops, w_ref, l_ref, r_ref, comb_ref, sector_ref, out_ref, density_ref,
     left, wide, main, rest, acc, mixed, coef, part_main, part_rest, from_main, from_rest,
     kept_main, kept_rest, away_main, away_rest, back_main, back_rest,
+    tile_main, tile_rest, mates_main, mates_rest, grams, turned, turned_out, turned_in, blocks_out, blocks_in,
     local_sem, send_sem, recv_sem, share_send, share_recv, x_send, x_recv, z_send, z_recv,
+    swap_send, swap_recv, turn_send, turn_recv, block_send, block_recv,
 ):
     zl, y, core, x, zh = (lax.axis_index(a) for a in AXES)
     gathered = (wide, main, rest)
@@ -152,12 +185,22 @@
         return (1 - zl if dz else zl) * 4 + ring(y, dy, 4)
 
     barrier = pltpu.get_barrier_semaphore()
-    partners = [*neighbour.values(), {"core": 1 - core}, {"zh": 1 - zh}]
-    partners += [{"x": ring(x, by, 4)} for by in (1, 2, 3)]
+    here = chip((0, 0)) * 2 + core
+    column = x * 2 + zh
+    partners = [*neighbour.values(), {"core": 1 - core}]
+    partners += [column_device(ring(column, by, 8)) for by in range(1, 8)]
     for partner in partners:
         pl.semaphore_signal(barrier, inc=1, device_id=partner, device_id_type=mesh_type)
-
-    here = chip((0, 0)) * 2 + core
+    mates = jnp.int32(0)
+    for offset in OFFSETS:
+        mates += inside(here + offset).astype(jnp.int32)
+
+        @pl.when(inside(here + offset))
+        def _(offset=offset):
+            pl.semaphore_signal(
+                barrier, inc=1, device_id=row_device(here + offset), device_id_type=mesh_type
+            )
+
     loads = [
         pltpu.make_async_copy(w_ref, wide.at[here], local_sem.at[0]),
         pltpu.make_async_copy(r_ref.at[:, 0:MAIN], main.at[here], local_sem.at[1]),
@@ -167,18 +210,18 @@
     for load in loads:
         load.start()
     row = lax.broadcasted_iota(jnp.int32, (256, 32), 0)
-    column = lax.broadcasted_iota(jnp.int32, (256, 32), 1)
-    spread = (row // 8 == column).astype(BF16)
+    lane_at = lax.broadcasted_iota(jnp.int32, (256, 32), 1)
+    spread = (row // 8 == lane_at).astype(BF16)
     row = lax.broadcasted_iota(jnp.int32, (256, 256), 0)
-    column = lax.broadcasted_iota(jnp.int32, (256, 256), 1)
-    same = row % 8 == column % 8
+    lane_at = lax.broadcasted_iota(jnp.int32, (256, 256), 1)
+    same = row % 8 == lane_at % 8
     high = comb_ref[...].astype(BF16)
     low = (comb_ref[...] - high.astype(F32)).astype(BF16)
     for at, term in enumerate((high, low)):
         tall = jnp.dot(spread, term, preferred_element_type=F32).astype(BF16)
         full = lax.dot_general(tall, spread, (((1,), (1,)), ((), ())), preferred_element_type=F32)
         coef[at * 256 : at * 256 + 256] = jnp.where(same, full, 0.0).astype(BF16)
-    pl.semaphore_wait(barrier, len(partners))
+    pl.semaphore_wait(barrier, len(partners) + mates)
     for load in loads:
         load.wait()
 
@@ -217,15 +260,19 @@
             device_id={"core": 1 - core}, device_id_type=mesh_type,
         )
 
-    def first(source, fresh):
-        k = chip(source)
-        columns = pl.ds(pl.multiple_of(k * 384, 384), 384)
+    def first(group, fresh):
+        chips = [chip(source) for source in group]
+        columns = [pl.ds(pl.multiple_of(k * 384, 384), 384) for k in chips]
 
         @pl.loop(0, 6)
         def _(tile):
             lanes = pl.ds(pl.multiple_of(tile * 256, 256), 256)
-            block = wide[pl.ds(k * 2, 2), :, lanes].reshape(384, 256)
-            product = jnp.dot(left[:, columns], block, preferred_element_type=F32)
+            block = [wide[pl.ds(k * 2, 2), :, lanes].reshape(384, 256) for k in chips]
+            rows = [left[:, c] for c in columns]
+            product = jnp.dot(
+                jnp.concatenate(rows, axis=1), jnp.concatenate(block, axis=0),
+                preferred_element_type=F32,
+            )
             if fresh:
                 acc[:, lanes] = product
             else:
@@ -275,18 +322,15 @@
         k = chip(source)
         width = 2 * SHARD[phase]
 
-        @pl.loop(0, 4)
-        def _(tile):
-            rows = pl.ds(pl.multiple_of(tile * 128, 128), 128)
-            total = None
-            for v in range(8):
-                block = gathered[phase][pl.ds(k * 2, 2), v].reshape(width, 384)
-                product = lax.dot_general(
-                    mixed[rows, v * 384 : v * 384 + 384], block,
-                    (((1,), (1,)), ((), ())), preferred_element_type=F32,
-                )
-                total = product if total is None else total + product
-            parts[phase][k, rows] = total.astype(BF16)
+        total = None
+        for v in range(0, 8, 2):
+            block = [gathered[phase][pl.ds(k * 2, 2), v + j].reshape(width, 384) for j in (0, 1)]
+            product = lax.dot_general(
+                mixed[:, v * 384 : v * 384 + 768], jnp.concatenate(block, axis=1),
+                (((1,), (1,)), ((), ())), preferred_element_type=F32,
+            )
+            total = product if total is None else total + product
+        parts[phase][k] = total.astype(BF16)
 
         copy, away = to_owner(phase, k)
 
@@ -316,25 +360,155 @@
                 total += froms[phase][half, slot, rows].astype(F32)
             put(rows, total)
 
-    def sum_parts(phase):
-        def put_away(rows, total):
+    def sum_away(phase):
+        def put(rows, total):
             aways[phase][rows] = total.astype(BF16)
 
-        def put_kept(rows, total):
+        sum_x(phase, 1 - zh, put)
+        z_copy(phase).start()
+
+    def sum_keep(phase):
+        def put(rows, total):
             keeps[phase][rows] = total
 
-        sum_x(phase, 1 - zh, put_away)
-        z_copy(phase).start()
-        sum_x(phase, zh, put_kept)
+        sum_x(phase, zh, put)
+
+    tiles = (None, tile_main, tile_rest)
+    mates_of = (None, mates_main, mates_rest)
 
     def finish(phase):
         z_copy(phase).wait_recv()
-        start, width = (0, 2 * MAIN) if phase == 1 else (2 * MAIN, 2 * REST)
         for site in range(4):
             rows = slice(site * 128, site * 128 + 128)
             value = keeps[phase][rows] + backs[phase][rows].astype(F32)
-            out_ref[site, :, start : start + width] = value.astype(BF16)
-
+            keeps[phase][rows] = value
+            tiles[phase][site] = value.astype(BF16)
+
+    def swap(phase, offset):
+        half, at = int(offset > 0), abs(offset) - 1
+        slot = ((phase - 1) * 2 + half) * 3 + at
+        return pltpu.make_async_remote_copy(
+            tiles[phase].at[pl.ds(half * 2, 2)], mates_of[phase].at[half, at],
+            swap_send.at[slot], swap_recv.at[slot],
+            device_id=row_device(here + offset), device_id_type=mesh_type,
+        )
+
+    def swaps(phase):
+        for offset in OFFSETS:
+
+            @pl.when(inside(here + offset))
+            def _(offset=offset):
+                swap(phase, offset).start()
+
+    def nt(a, b):
+        return lax.dot_general(a, b, (((1,), (1,)), ((), ())), preferred_element_type=F32)
+
+    def gram(phase):
+        width = 2 * SHARD[phase]
+        for offset in OFFSETS:
+
+            @pl.when(inside(here - offset))
+            def _(offset=offset):
+                swap(phase, offset).wait_recv()
+
+        own = sum(nt(tiles[phase][site], tiles[phase][site]) for site in range(4))
+        straight, crossed = [], []
+        for half in (0, 1):
+            mine = [tiles[phase][half * 2 + j] for j in (0, 1)]
+            theirs = [mates_of[phase][half, :, j].reshape(384, width) for j in (0, 1)]
+            straight.append(sum(nt(a, b) for a, b in zip(mine, theirs)))
+            crossed.append(sum(nt(b, a) for a, b in zip(mine, theirs)))
+        if phase == 1:
+            grams[2, :, 0:128] = own
+            for half in (0, 1):
+                grams[half] = straight[half]
+                turned[half] = crossed[half]
+        else:
+            grams[2, :, 0:128] += own
+            for half in (0, 1):
+                grams[half] += straight[half]
+                turned_out[half] = (turned[half] + crossed[half]).astype(BF16)
+
+    def turn(offset):
+        half, at = int(offset < 0), abs(offset) - 1
+        return pltpu.make_async_remote_copy(
+            turned_out.at[half, pl.ds(at * 128, 128)], turned_in.at[1 - half, pl.ds(at * 128, 128)],
+            turn_send.at[half * 3 + at], turn_recv.at[half * 3 + at],
+            device_id=row_device(here + offset), device_id_type=mesh_type,
+        )
+
+    def block_copy(offset):
+        mate = here + offset
+        owner, half = mate // 2, lax.rem(mate, 2)
+        return pltpu.make_async_remote_copy(
+            blocks_out.at[offset + 3], blocks_in.at[half, column],
+            block_send.at[offset + 3], block_recv.at[half * 8 + column],
+            device_id=column_device(owner), device_id_type=mesh_type,
+        )
+
+    def reach():
+        for offset in OFFSETS:
+
+            @pl.when(inside(here + offset))
+            def _(offset=offset):
+                turn(offset).start()
+
+        for offset in (0, *OFFSETS):
+            half, at = int(offset < 0), abs(offset) - 1
+
+            @pl.when(inside(here + offset))
+            def _(offset=offset, half=half, at=at):
+                if offset:
+                    turn(-offset).wait_recv()
+                    came = turned_in[half, at * 128 : at * 128 + 128].astype(F32)
+                    value = grams[half, :, at * 128 : at * 128 + 128] + came
+                else:
+                    value = grams[2, :, 0:128]
+                owner = (here + offset) // 2
+
+                @pl.when(owner == column)
+                def _():
+                    blocks_in[lax.rem(here + offset, 2), column] = value.astype(BF16)
+
+                @pl.when(owner != column)
+                def _():
+                    blocks_out[offset + 3] = value.astype(BF16)
+                    block_copy(offset).start()
+
+        for half in (0, 1):
+            mate = column * 2 + half
+            near = jnp.logical_and(mate - here <= 3, here - mate <= 3)
+            lanes = slice(half * 128, half * 128 + 128)
+
+            @pl.when(near)
+            def _(half=half, mate=mate, lanes=lanes):
+                for by in range(1, 8):
+                    source = ring(column, by, 8)
+                    pltpu.make_async_remote_copy(
+                        blocks_out.at[0], blocks_in.at[half, source],
+                        block_send.at[0], block_recv.at[half * 8 + source],
+                        device_id=column_device(source), device_id_type=mesh_type,
+                    ).wait_recv()
+                total = sum(blocks_in[half, n].astype(F32) for n in range(8))
+                same_sector = sector_ref[mate] == sector_ref[here]
+                total = total * (1.0 / math.sqrt(4.0 * BOND_WIDTH))
+                density_ref[:, lanes] = jnp.where(same_sector, total, 0.0)
+
+            @pl.when(jnp.logical_not(near))
+            def _(lanes=lanes):
+                density_ref[:, lanes] = jnp.zeros((128, 128), F32)
+
+    def write_out():
+        lane = lax.broadcasted_iota(jnp.int32, (128, 128), 1)
+        for site in range(4):
+            rows = slice(site * 128, site * 128 + 128)
+            out_ref[site, :, 0:128] = tile_main[site, :, 0:128]
+            rolled = pltpu.roll(kept_main[rows, 128:256], 64, 1)
+            last = kept_rest[rows, :]
+            out_ref[site, :, 128:256] = jnp.where(lane < 64, last, rolled).astype(BF16)
+            out_ref[site, :, 256:384] = jnp.where(lane < 64, rolled, last).astype(BF16)
+
+    after = dict(away=sum_away, keep=sum_keep, finish=finish, swap=swaps, gram=gram)
     for phase in range(3):
         share(phase, (0, 0), core).start()
     for op in ops:
@@ -347,17 +521,19 @@
         elif op[0] == "share":
             share(op[1], op[2], core).start()
         elif op[0] == "first":
-            share(0, op[1], 1 - core).wait_recv()
+            for source in op[1]:
+                share(0, source, 1 - core).wait_recv()
             first(op[1], op[2])
         elif op[0] == "mix":
             mix(op[1])
         elif op[0] == "second":
             share(op[1], op[2], 1 - core).wait_recv()
             second(op[1], op[2])
-        elif op[0] == "sum":
-            sum_parts(op[1])
-    for phase in (1, 2):
-        finish(phase)
+        else:
+            if op == ("gram", 2):
+                write_out()
+            after[op[0]](op[1])
+    reach()
     for copy in sent:
         copy.wait_send()
     for phase in range(3):
@@ -372,8 +548,22 @@
             def _(copy=copy):
                 copy.wait_send()
 
-
-def applied_of(wavefunction, left_environment, combined, right_environment):
+    for offset in OFFSETS:
+
+        @pl.when(inside(here + offset))
+        def _(offset=offset):
+            swap(1, offset).wait_send()
+            swap(2, offset).wait_send()
+            turn(offset).wait_send()
+
+    for offset in (0, *OFFSETS):
+
+        @pl.when(jnp.logical_and(inside(here + offset), (here + offset) // 2 != column))
+        def _(offset=offset):
+            block_copy(offset).wait_send()
+
+
+def fused(wavefunction, left_environment, combined, right_environment, row_sector):
     ops, _ = schedule()
     vmem = pltpu.VMEM
     dma = pltpu.SemaphoreType.DMA
@@ -385,15 +575,22 @@
         vmem((2, 3, 512, 256), BF16), vmem((2, 3, 512, 128), BF16),
         vmem((512, 256), F32), vmem((512, 128), F32), vmem((512, 256), BF16), vmem((512, 128), BF16),
         vmem((512, 256), BF16), vmem((512, 128), BF16),
+        vmem((4, 128, 256), BF16), vmem((4, 128, 128), BF16), vmem((2, 3, 2, 128, 256), BF16),
+        vmem((2, 3, 2, 128, 128), BF16), vmem((3, 128, 384), F32), vmem((2, 384, 128), F32),
+        vmem((2, 384, 128), BF16), vmem((2, 384, 128), BF16), vmem((7, 128, 128), BF16),
+        vmem((2, 8, 128, 128), BF16),
         dma((4,)), dma((count,)), dma((count,)), dma((24,)), dma((24,)), dma((16,)), dma((12,)),
-        dma((2,)), dma((2,)),
+        dma((2,)), dma((2,)), dma((12,)), dma((12,)), dma((6,)), dma((6,)), dma((7,)), dma((16,)),
     ]
     spec = pl.BlockSpec(memory_space=pl.ANY)
     return pl.pallas_call(
         functools.partial(kernel, ops),
-        out_shape=jax.ShapeDtypeStruct((4, 128, 384), BF16),
-        in_specs=[spec, spec, spec, pl.BlockSpec(memory_space=pltpu.VMEM)],
-        out_specs=pl.BlockSpec(memory_space=pltpu.VMEM),
+        out_shape=(
+            jax.ShapeDtypeStruct((4, 128, 384), BF16), jax.ShapeDtypeStruct((128, 256), F32)
+        ),
+        in_specs=[spec, spec, spec, pl.BlockSpec(memory_space=pltpu.VMEM),
+                  pl.BlockSpec(memory_space=pltpu.SMEM)],
+        out_specs=(pl.BlockSpec(memory_space=pltpu.VMEM),) * 2,
         scratch_shapes=scratch,
         compiler_params=pltpu.CompilerParams(
             collective_id=0, has_side_effects=True, vmem_limit_bytes=61 << 20
@@ -403,6 +600,7 @@
         left_environment.reshape(1024, 3072),
         right_environment.transpose(0, 2, 1),
         combined,
+        row_sector,
     )
 
 
@@ -414,70 +612,14 @@
     return joined.reshape(4 * channels, 4 * channels)
 
 
-def split_up(value, dim, devices):
-    before, after = (value.shape[:dim], value.shape[dim + 1 :])
-    return jnp.moveaxis(value.reshape(*before, devices, -1, *after), dim, 0)
-
-
-def sent_and_summed(value, axis, dim):
-    parts = split_up(value, dim, lax.axis_size(axis))
-    arrived = lax.all_to_all(parts, axis, split_axis=0, concat_axis=0, tiled=True)
-    return arrived.astype(jnp.float32).sum(axis=0)
-
-
-def shifted(value, axis, by):
-    devices = lax.axis_size(axis)
-    pairs = [(i, i + by) for i in range(devices) if 0 <= i + by < devices]
-    return lax.ppermute(value, axis, pairs)
-
-
-def label_at(labels, position):
-    matches = jnp.arange(labels.shape[0], dtype=jnp.int32) == position
-    return (jnp.sum(jnp.where(matches, labels, 0)), jnp.any(matches))
-
-
-def tile_gram(left_tile, right_tile):
-    return lax.dot_general(
-        left_tile, right_tile, (((1,), (1,)), ((), ())), preferred_element_type=jnp.float32
-    )
-
-
 def shards(
     wavefunction, left_environment, operator_left, operator_right, right_environment, row_sector
 ):
     combined = combine_operators(operator_left, operator_right)
-    raw = applied_of(wavefunction, left_environment, combined, right_environment)
-    raw = raw.transpose(1, 0, 2)
-    applied = jnp.concatenate(
-        [raw[..., 0:128], raw[..., 256:320], raw[..., 128:256], raw[..., 320:384]], axis=2
+    raw, density = fused(
+        wavefunction, left_environment, combined, right_environment, row_sector
     )
-    row_count = 128
-    own_tile = applied.reshape(row_count, 4 * 384)
-    own_index = lax.axis_index(LB)
-    tile_count = 16
-    reach_tiles = SECTOR_TILES - 1
-    own_label = label_at(row_sector, own_index)[0]
-    buffer = jnp.zeros((row_count, (tile_count + 2 * reach_tiles) * row_count), jnp.float32)
-
-    def place_block(buffer, gram_block, offset):
-        mate_index = own_index + offset
-        mate_label, inside = label_at(row_sector, mate_index)
-        keep_block = jnp.logical_and(inside, mate_label == own_label)
-        gram_block = jnp.where(keep_block, gram_block, jnp.float32(0.0))
-        column_start = (mate_index + reach_tiles) * row_count
-        return lax.dynamic_update_slice(buffer, gram_block, (jnp.int32(0), column_start))
-
-    buffer = place_block(buffer, tile_gram(own_tile, own_tile), 0)
-    for distance in range(1, SECTOR_TILES):
-        gram_block = tile_gram(own_tile, shifted(own_tile, LB, -distance))
-        buffer = place_block(buffer, gram_block, distance)
-        returned = shifted(gram_block.astype(jnp.bfloat16), LB, distance).astype(gram_block.dtype)
-        buffer = place_block(buffer, returned.T, -distance)
-    full_rows = buffer[:, reach_tiles * row_count : (reach_tiles + tile_count) * row_count]
-    density = sent_and_summed(full_rows.astype(jnp.bfloat16), RB, 1) * (
-        1.0 / math.sqrt(4.0 * BOND_WIDTH)
-    )
-    return (applied, density)
+    return raw.transpose(1, 0, 2), density
 
 
 def solution(mesh):

time: 208 us -> 162 us (0.78)
  starting transfers between devices: 25.6 us -> 0 us
  Pallas kernels: 138 us -> 152 us
  waiting for transfers between devices: 12.6 us -> 0 us
  between operations: 12.1 us -> 0.66 us
  other arithmetic: 5.5 us -> 0 us
    ppermute x6 -> x0, starting transfers between devices: 18.5 us -> none  [shifted(): return lax.ppermute(value, axis, pairs)]
    pallas_call x1, Pallas kernels: 138 us -> 152 us  [fused(): pl.pallas_call(functools.partial(kernel, ops), out_shape=(jax.ShapeDtypeS...]
    all_to_all x1 -> x0, waiting for transfers between devices: 9.07 us -> none  [sent_and_summed(): lax.all_to_all(parts, axis, split_axis=0, concat_axis=0, tiled=True)]
    all_to_all x1 -> x0, starting transfers between devices: 7.03 us -> none  [sent_and_summed(): lax.all_to_all(parts, axis, split_axis=0, concat_axis=0, tiled=True)]
    reduce_or x7 -> x0, other arithmetic: 4.44 us -> none  [label_at(): return (jnp.sum(jnp.where(matches, labels, 0)), jnp.any(matches))]
    ppermute x6 -> x0, waiting for transfers between devices: 3.53 us -> none  [shifted(): return lax.ppermute(value, axis, pairs)]
    slice x3 -> x0, local copies, waits for them, and re-layouts: 2.93 us -> none  [the longest x1 1.11 us: shards(): raw[..., 256:320]]
    unnamed x7 -> x5, local copies, waits for them, and re-layouts: 3.77 us -> 6.28 us
  transfers between devices with their start and end apart: 7 -> 0, of which waited for: 2 -> 0; matrix products, arithmetic and copies ran while one was open for 4% -> 0% of each run, Pallas kernels for 0% -> 0%
where the time goes in v2:
time: 162 us; the launch traced here: 161 us
  Pallas kernels  152 us (94%)
  local copies, waits for them, and re-layouts  7.7 us (5%)
    pallas_call x1, Pallas kernels, fused(): pl.pallas_call(functools.partial(kernel, ops), out_shape=(jax.ShapeDtypeS...  152 us
    unnamed x5, local copies, waits for them, and re-layouts  6.28 us

profile of v2, /device:TPU:9, one launch (start us, length us, event | category | flops | bytes accessed | tf_op | source)
XLA Modules:
  0.0 161.3 jit_solution(15686357472497720155)
XLA Ops:
  0.6 0.0 copy-start
  0.6 0.7 copy-done
  1.4 1.1 convolution_bitcast_fusion
  2.5 0.5 copy.14
  2.9 1.0 reshape.15.comb_ref
  3.9 1.9 %copy.22 = bf16[24,8,4,384]{3,1,2,0:T(8,128)(2,1)} copy(bf16[24,8,4,384]{3,2,1,0:T(4,128)(2,1)} %bitcast.13) | data formatting | bytes 1179648
  5.9 151.8 %shard_map.77 = (bf16[4,128,384]{2,1,0:T(8,128)(2,1)}, f32[128,256]{1,0:T(8,128)}) custom-call(bf16[192,1536]{1,0:T(8,128)(2,1)} %bitcast.11, bf16[1024,3072]{1,0:T(8,128)(2,1)} %bitcast.10, bf16[8,192,384]{2,1,0:T(8,128)(2,1)} %bitcast.12, f32[32,32]{1,0:T(8,128)} %reshape.15.comb_ref, s32[16]{0:T(128)} %sector_ref.1), custom_call_target="tpu_custom_call" | custom-call | tf_op jit(solution)/shard_map/pallas_call | solution.py:586
  157.7 2.0 %copy.15 = bf16[128,4,384]{2,1,0:T(4,128)(2,1)} copy(bf16[128,4,384]{2,0,1:T(8,128)(2,1)} %bitcast.14) | data formatting | bytes 786432
  159.7 1.6 copy.28
Async XLA Ops:
  0.6 0.7 copy-start

commit v3 on v2

--- a/solution.py
+++ b/solution.py
@@ -20,7 +20,7 @@
 PIECES = (
     (("z", 1, 0, 64), ("z", -1, 64, 48), ("y", 1, 112, 32), ("y", -1, 144, 48)),
     (("z", 1, 0, 32), ("z", -1, 32, 32), ("y", 1, 64, 32), ("y", -1, 96, 32)),
-    (("z", 1, 0, 32), ("z", -1, 32, 16), ("y", -1, 48, 16)),
+    (("z", 1, 0, 16), ("z", -1, 16, 16), ("y", 1, 32, 16), ("y", -1, 48, 16)),
 )
 UNIT_BYTES = (1536 * 2, 8 * 384 * 2, 8 * 384 * 2)
 SHARD = (192, MAIN, REST)
@@ -110,12 +110,16 @@
         able = [k for k, at in ready.items() if at is not None and at <= now and k not in done]
         group = FIRSTS[firsts] if firsts < len(FIRSTS) else None
         due = [entry for entry in later if entry[0] <= now]
-        if group is not None:
+        if due and due[0][1] == "first":
+            later.remove(due[0])
+            ops.append((now, *due[0][1:]))
+            tc_free = now + 0.4 + 0.6 * len(due[0][2])
+        elif group is not None:
             if all((0, source) in able for source in group):
                 done.update((0, source) for source in group)
-                ops.append((now, "first", group, firsts == 0))
+                for part in (0, 1):
+                    later.append((now, "first", group, firsts == 0, part))
                 firsts += 1
-                tc_free = now + 1.0 + 1.1 * len(group)
         elif mixes < 4:
             ops.append((now, "mix", mixes))
             mixes += 1
@@ -163,7 +167,7 @@
 
 
 def kernel(
-    ops, w_ref, l_ref, r_ref, comb_ref, sector_ref, out_ref, density_ref,
+    ops, w_ref, l_ref, r_ref, ol_ref, or_ref, sector_ref, out_ref, density_ref,
     left, wide, main, rest, acc, mixed, coef, part_main, part_rest, from_main, from_rest,
     kept_main, kept_rest, away_main, away_rest, back_main, back_rest,
     tile_main, tile_rest, mates_main, mates_rest, grams, turned, turned_out, turned_in, blocks_out, blocks_in,
@@ -209,20 +213,8 @@
     ]
     for load in loads:
         load.start()
-    row = lax.broadcasted_iota(jnp.int32, (256, 32), 0)
-    lane_at = lax.broadcasted_iota(jnp.int32, (256, 32), 1)
-    spread = (row // 8 == lane_at).astype(BF16)
-    row = lax.broadcasted_iota(jnp.int32, (256, 256), 0)
-    lane_at = lax.broadcasted_iota(jnp.int32, (256, 256), 1)
-    same = row % 8 == lane_at % 8
-    high = comb_ref[...].astype(BF16)
-    low = (comb_ref[...] - high.astype(F32)).astype(BF16)
-    for at, term in enumerate((high, low)):
-        tall = jnp.dot(spread, term, preferred_element_type=F32).astype(BF16)
-        full = lax.dot_general(tall, spread, (((1,), (1,)), ((), ())), preferred_element_type=F32)
-        coef[at * 256 : at * 256 + 256] = jnp.where(same, full, 0.0).astype(BF16)
     pl.semaphore_wait(barrier, len(partners) + mates)
-    for load in loads:
+    for load in loads[:3]:
         load.wait()
 
     sent = []
@@ -260,11 +252,44 @@
             device_id={"core": 1 - core}, device_id_type=mesh_type,
         )
 
-    def first(group, fresh):
+    def coefficients():
+        def of(size, dim):
+            return lax.broadcasted_iota(jnp.int32, size, dim)
+
+        def dot(a, b, dims=(((1,), (0,)), ((), ()))):
+            return lax.dot_general(
+                a, b, dims, precision=lax.Precision.HIGHEST, preferred_element_type=F32
+            )
+
+        across = (((1,), (1,)), ((), ()))
+        tall, short = of((256, 32), 0), of((256, 32), 1)
+        pick = (of((256, 8), 0) // 32 == of((256, 8), 1)).astype(F32)
+        right = dot(pick, or_ref[...].reshape(32, 8), across)
+        right = jnp.where(tall // 8 % 2 == short // 2 % 2, right, 0.0)
+        i, j = of((32, 32), 0), of((32, 32), 1)
+        right = dot(right, jnp.logical_and(i // 4 == j // 4, i % 2 == j % 2).astype(F32))
+        right = jnp.where(tall // 16 % 2 == short // 2 % 2, right, 0.0)
+        lefts = ol_ref[...].reshape(32, 8)
+        total = None
+        for site in (0, 1):
+            wanted = jnp.logical_and(tall // 32 == short // 4, tall // 16 % 2 == short % 2)
+            wanted = jnp.logical_and(wanted, short // 2 % 2 == site).astype(F32)
+            i, j = of((8, 32), 0), of((8, 32), 1)
+            place = jnp.logical_and(i == j // 4, j // 2 % 2 == site).astype(F32)
+            term = dot(dot(wanted, lefts), place)
+            total = term if total is None else total + term
+        total = jnp.where(tall // 8 % 2 == short % 2, total, 0.0)
+        full = dot(right, total, across)
+        full = jnp.where(of((256, 256), 0) % 8 == of((256, 256), 1) % 8, full, 0.0)
+        high = full.astype(BF16)
+        coef[0:256] = high
+        coef[256:512] = (full - high.astype(F32)).astype(BF16)
+
+    def first(group, fresh, part):
         chips = [chip(source) for source in group]
         columns = [pl.ds(pl.multiple_of(k * 384, 384), 384) for k in chips]
 
-        @pl.loop(0, 6)
+        @pl.loop(part * 3, part * 3 + 3)
         def _(tile):
             lanes = pl.ds(pl.multiple_of(tile * 256, 256), 256)
             block = [wide[pl.ds(k * 2, 2), :, lanes].reshape(384, 256) for k in chips]
@@ -512,6 +537,8 @@
     for phase in range(3):
         share(phase, (0, 0), core).start()
     for op in ops:
+        if op[0] == "first" and op[2] and not op[3]:
+            coefficients()
         if op[0] == "send":
             send(op[1], op[2], (0, 0))
         elif op[0] == "take":
@@ -521,9 +548,12 @@
         elif op[0] == "share":
             share(op[1], op[2], core).start()
         elif op[0] == "first":
-            for source in op[1]:
-                share(0, source, 1 - core).wait_recv()
-            first(op[1], op[2])
+            if not op[3]:
+                for source in op[1]:
+                    share(0, source, 1 - core).wait_recv()
+            if op[2] and not op[3]:
+                loads[3].wait()
+            first(*op[1:])
         elif op[0] == "mix":
             mix(op[1])
         elif op[0] == "second":
@@ -563,7 +593,7 @@
             block_copy(offset).wait_send()
 
 
-def fused(wavefunction, left_environment, combined, right_environment, row_sector):
+def fused(wavefunction, left_environment, operator_left, operator_right, right_environment, row_sector):
     ops, _ = schedule()
     vmem = pltpu.VMEM
     dma = pltpu.SemaphoreType.DMA
@@ -588,8 +618,8 @@
         out_shape=(
             jax.ShapeDtypeStruct((4, 128, 384), BF16), jax.ShapeDtypeStruct((128, 256), F32)
         ),
-        in_specs=[spec, spec, spec, pl.BlockSpec(memory_space=pltpu.VMEM),
-                  pl.BlockSpec(memory_space=pltpu.SMEM)],
+        in_specs=[spec] * 3 + [pl.BlockSpec(memory_space=pltpu.VMEM)] * 2
+        + [pl.BlockSpec(memory_space=pltpu.SMEM)],
         out_specs=(pl.BlockSpec(memory_space=pltpu.VMEM),) * 2,
         scratch_shapes=scratch,
         compiler_params=pltpu.CompilerParams(
@@ -599,25 +629,17 @@
         wavefunction.reshape(192, 1536),
         left_environment.reshape(1024, 3072),
         right_environment.transpose(0, 2, 1),
-        combined,
+        operator_left.transpose(0, 2, 3, 1),
+        operator_right.transpose(0, 2, 3, 1),
         row_sector,
     )
-
-
-def combine_operators(operator_left, operator_right):
-    channels = operator_left.shape[0]
-    joined = jnp.einsum(
-        "aups,uvqt->vpqast", operator_left, operator_right, precision=lax.Precision.HIGHEST
-    )
-    return joined.reshape(4 * channels, 4 * channels)
 
 
 def shards(
     wavefunction, left_environment, operator_left, operator_right, right_environment, row_sector
 ):
-    combined = combine_operators(operator_left, operator_right)
     raw, density = fused(
-        wavefunction, left_environment, combined, right_environment, row_sector
+        wavefunction, left_environment, operator_left, operator_right, right_environment, row_sector
     )
     return raw.transpose(1, 0, 2), density
 

time: 162 us -> 158 us (0.975)
  local copies, waits for them, and re-layouts: 7.7 us -> 5.57 us
    unnamed x5 -> x3, local copies, waits for them, and re-layouts: 6.28 us -> 5.57 us
where the time goes in v3:
time: 158 us; the launch traced here: 157 us
  Pallas kernels  151 us (96%)
  local copies, waits for them, and re-layouts  5.57 us (4%)
    pallas_call x1, Pallas kernels, fused(): pl.pallas_call(functools.partial(kernel, ops), out_shape=(jax.ShapeDtypeS...  151 us
    unnamed x3, local copies, waits for them, and re-layouts  5.57 us

profile of v3, /device:TPU:9, one launch (start us, length us, event | category | flops | bytes accessed | tf_op | source)
XLA Modules:
  0.0 157.4 jit_solution(13645263649438752249)
XLA Ops:
  0.6 2.0 %copy.9 = bf16[24,8,4,384]{3,1,2,0:T(8,128)(2,1)} copy(bf16[24,8,4,384]{3,2,1,0:T(4,128)(2,1)} %bitcast.10) | data formatting | bytes 1179648
  2.6 151.2 %shard_map.77 = (bf16[4,128,384]{2,1,0:T(8,128)(2,1)}, f32[128,256]{1,0:T(8,128)}) custom-call(bf16[192,1536]{1,0:T(8,128)(2,1)} %bitcast.8, bf16[1024,3072]{1,0:T(8,128)(2,1)} %bitcast.7, bf16[8,192,384]{2,1,0:T(8,128)(2,1)} %bitcast.9, f32[8,2,2,8]{3,2,1,0:T(2,128)} %bitcast.12, f32[8,2,2,8]{3,2,1,0:T(2,128)} %bitcast.13, s32[16]{0:T(128)} %sector_ref.1), custom_call_target="tpu_custom_call" | custom-call | tf_op jit(solution)/shard_map/pallas_call | solution.py:616
  153.8 2.0 %copy.8 = bf16[128,4,384]{2,1,0:T(4,128)(2,1)} copy(bf16[128,4,384]{2,0,1:T(8,128)(2,1)} %bitcast.11) | data formatting | bytes 786432
  155.8 1.6 copy.11

commit v4 on v3

--- a/solution.py
+++ b/solution.py
@@ -20,7 +20,7 @@
 PIECES = (
     (("z", 1, 0, 64), ("z", -1, 64, 48), ("y", 1, 112, 32), ("y", -1, 144, 48)),
     (("z", 1, 0, 32), ("z", -1, 32, 32), ("y", 1, 64, 32), ("y", -1, 96, 32)),
-    (("z", 1, 0, 16), ("z", -1, 16, 16), ("y", 1, 32, 16), ("y", -1, 48, 16)),
+    (("z", 1, 0, 32), ("z", -1, 32, 16), ("y", -1, 48, 16)),
 )
 UNIT_BYTES = (1536 * 2, 8 * 384 * 2, 8 * 384 * 2)
 SHARD = (192, MAIN, REST)
@@ -61,7 +61,7 @@
             yield "-", (phase, piece, (0, 1))
 
 
-def schedule(rate=43.5e3, lag=1.0, lead=5.0, step=0.05):
+def schedule(rate=43.5e3, lag=1.0, lead=10.0, step=0.05):
     spent = (None, 1.1, 0.7)
     waiting = {link: [] for link in "+-z"}
     for order, (link, message) in enumerate(own_sends()):
@@ -139,8 +139,10 @@
                 for name, gap in LATER:
                     wait += gap
                     later.append((tc_free + wait, name, 1))
-    ops += [(now, *entry[1:]) for entry in later]
-    ops += [(now, name, 2) for name, _ in LATER]
+    rest = [entry[1] for entry in later]
+    ops += [(now, name, 1) for name in rest[:-1]]
+    ops += [(now, name, 2) for name, _ in LATER[:-1]]
+    ops += [(now, "gram", phase) for phase in ((1, 2) if rest else (2,))]
     for at, _, link, message in reversed(issued):
         place = next((i for i, op in enumerate(ops) if op[0] > at), len(ops))
         ops.insert(place, (at, "send", link, message))
@@ -168,7 +170,7 @@
 
 def kernel(
     ops, w_ref, l_ref, r_ref, ol_ref, or_ref, sector_ref, out_ref, density_ref,
-    left, wide, main, rest, acc, mixed, coef, part_main, part_rest, from_main, from_rest,
+    raw, left, wide, main, rest, acc, mixed, coef, part_main, part_rest, from_main, from_rest,
     kept_main, kept_rest, away_main, away_rest, back_main, back_rest,
     tile_main, tile_rest, mates_main, mates_rest, grams, turned, turned_out, turned_in, blocks_out, blocks_in,
     local_sem, send_sem, recv_sem, share_send, share_recv, x_send, x_recv, z_send, z_recv,
@@ -206,16 +208,18 @@
             )
 
     loads = [
-        pltpu.make_async_copy(w_ref, wide.at[here], local_sem.at[0]),
+        pltpu.make_async_copy(w_ref, raw, local_sem.at[0]),
         pltpu.make_async_copy(r_ref.at[:, 0:MAIN], main.at[here], local_sem.at[1]),
         pltpu.make_async_copy(r_ref.at[:, MAIN : MAIN + REST], rest.at[here], local_sem.at[2]),
         pltpu.make_async_copy(l_ref, left, local_sem.at[3]),
     ]
     for load in loads:
         load.start()
+    loads[0].wait()
+    wide[here] = raw[...].reshape(192, 1536)
+    loads[1].wait()
+    loads[2].wait()
     pl.semaphore_wait(barrier, len(partners) + mates)
-    for load in loads[:3]:
-        load.wait()
 
     sent = []
 
@@ -418,6 +422,9 @@
             device_id=row_device(here + offset), device_id_type=mesh_type,
         )
 
+    def nt(a, b):
+        return lax.dot_general(a, b, (((1,), (1,)), ((), ())), preferred_element_type=F32)
+
     def swaps(phase):
         for offset in OFFSETS:
 
@@ -425,34 +432,34 @@
             def _(offset=offset):
                 swap(phase, offset).start()
 
-    def nt(a, b):
-        return lax.dot_general(a, b, (((1,), (1,)), ((), ())), preferred_element_type=F32)
+        tile = jnp.concatenate([tiles[phase][site] for site in range(4)], axis=1)
+        own = nt(tile, tile)
+        grams[2, :, 0:128] = own if phase == 1 else grams[2, :, 0:128] + own
 
     def gram(phase):
         width = 2 * SHARD[phase]
-        for offset in OFFSETS:
-
-            @pl.when(inside(here - offset))
-            def _(offset=offset):
-                swap(phase, offset).wait_recv()
-
-        own = sum(nt(tiles[phase][site], tiles[phase][site]) for site in range(4))
-        straight, crossed = [], []
         for half in (0, 1):
-            mine = [tiles[phase][half * 2 + j] for j in (0, 1)]
+            for offset in OFFSETS[3 - 3 * half :][:3]:
+
+                @pl.when(inside(here - offset))
+                def _(offset=offset):
+                    swap(phase, offset).wait_recv()
+
+            mine = jnp.concatenate([tiles[phase][half * 2 + j] for j in (0, 1)], axis=1)
             theirs = [mates_of[phase][half, :, j].reshape(384, width) for j in (0, 1)]
-            straight.append(sum(nt(a, b) for a, b in zip(mine, theirs)))
-            crossed.append(sum(nt(b, a) for a, b in zip(mine, theirs)))
-        if phase == 1:
-            grams[2, :, 0:128] = own
-            for half in (0, 1):
-                grams[half] = straight[half]
-                turned[half] = crossed[half]
-        else:
-            grams[2, :, 0:128] += own
-            for half in (0, 1):
-                grams[half] += straight[half]
-                turned_out[half] = (turned[half] + crossed[half]).astype(BF16)
+            theirs = jnp.concatenate(theirs, axis=1)
+            straight, crossed = nt(mine, theirs), nt(theirs, mine)
+            if phase == 1:
+                grams[half] = straight
+                turned[half] = crossed
+            else:
+                turned_out[half] = (turned[half] + crossed).astype(BF16)
+                grams[half] += straight
+                for offset in OFFSETS[3 * half :][:3]:
+
+                    @pl.when(inside(here + offset))
+                    def _(offset=offset):
+                        turn(offset).start()
 
     def turn(offset):
         half, at = int(offset < 0), abs(offset) - 1
@@ -472,12 +479,6 @@
         )
 
     def reach():
-        for offset in OFFSETS:
-
-            @pl.when(inside(here + offset))
-            def _(offset=offset):
-                turn(offset).start()
-
         for offset in (0, *OFFSETS):
             half, at = int(offset < 0), abs(offset) - 1
 
@@ -599,7 +600,7 @@
     dma = pltpu.SemaphoreType.DMA
     count = len(MESSAGES)
     scratch = [
-        vmem((1024, 3072), BF16), vmem((16, 192, 1536), BF16), vmem((16, 8, MAIN, 384), BF16),
+        vmem((192, 4, 384), BF16), vmem((1024, 3072), BF16), vmem((16, 192, 1536), BF16), vmem((16, 8, MAIN, 384), BF16),
         vmem((16, 8, REST, 384), BF16), vmem((1024, 1536), F32), vmem((512, 3072), BF16),
         vmem((512, 256), BF16), vmem((8, 512, 256), BF16), vmem((8, 512, 128), BF16),
         vmem((2, 3, 512, 256), BF16), vmem((2, 3, 512, 128), BF16),
@@ -615,9 +616,7 @@
     spec = pl.BlockSpec(memory_space=pl.ANY)
     return pl.pallas_call(
         functools.partial(kernel, ops),
-        out_shape=(
-            jax.ShapeDtypeStruct((4, 128, 384), BF16), jax.ShapeDtypeStruct((128, 256), F32)
-        ),
+        out_shape=(pltpu.VMEM((4, 128, 384), BF16), pltpu.VMEM((128, 256), F32)),
         in_specs=[spec] * 3 + [pl.BlockSpec(memory_space=pltpu.VMEM)] * 2
         + [pl.BlockSpec(memory_space=pltpu.SMEM)],
         out_specs=(pl.BlockSpec(memory_space=pltpu.VMEM),) * 2,
@@ -626,7 +625,7 @@
             collective_id=0, has_side_effects=True, vmem_limit_bytes=61 << 20
         ),
     )(
-        wavefunction.reshape(192, 1536),
+        wavefunction,
         left_environment.reshape(1024, 3072),
         right_environment.transpose(0, 2, 1),
         operator_left.transpose(0, 2, 3, 1),

time: 158 us -> 152 us (0.962)
  local copies, waits for them, and re-layouts: 5.57 us -> 1.71 us
  Pallas kernels: 151 us -> 148 us
    unnamed x3 -> x2, local copies, waits for them, and re-layouts: 5.57 us -> 1.71 us
    pallas_call x1, Pallas kernels: 151 us -> 148 us  [fused(): pl.pallas_call(functools.partial(kernel, ops), out_shape=(pltpu.VMEM((4,...]
where the time goes in v4:
time: 152 us; the launch traced here: 150 us
  Pallas kernels  148 us (97%)
  local copies, waits for them, and re-layouts  1.71 us (1%)
    pallas_call x1, Pallas kernels, fused(): pl.pallas_call(functools.partial(kernel, ops), out_shape=(pltpu.VMEM((4,...  148 us

profile of v4, /device:TPU:9, one launch (start us, length us, event | category | flops | bytes accessed | tf_op | source)
XLA Modules:
  0.0 149.9 jit_solution(18346011625010148276)
XLA Ops:
  0.6 147.5 %shard_map.77 = (bf16[4,128,384]{2,1,0:T(8,128)(2,1)S(1)}, f32[128,256]{1,0:T(8,128)S(1)}) custom-call(bf16[192,4,384]{2,1,0:T(4,128)(2,1)} %w_ref.1, bf16[1024,3072]{1,0:T(8,128)(2,1)} %bitcast.6, bf16[8,192,384]{2,1,0:T(8,128)(2,1)} %bitcast.7, f32[8,2,2,8]{3,2,1,0:T(2,128)} %bitcast.8, f32[8,2,2,8]{3,2,1,0:T(2,128)} %bitcast.9, s32[16]{0:T(128)} %sector_ref.1), custom_call_target="tpu_custom_call" | custom-call | tf_op jit(solution)/shard_map/pallas_call | solution.py:617
  148.2 1.1 copy.8
  149.2 0.7 copy.10

commit v5 on v4

--- a/solution.py
+++ b/solution.py
@@ -34,7 +34,7 @@
 
 
 FIRSTS = (((0, 0),), ((0, 1), (0, 3)), ((1, 0),), ((1, 1), (1, 3)), ((0, 2), (1, 2)))
-LATER = (("away", 10.0), ("keep", 1.0), ("finish", 6.0), ("swap", 0.5), ("gram", 9.0))
+LATER = (("away", 15.0), ("keep", 1.0), ("finish", 6.0), ("swap", 0.5), ("gram", 9.0))
 
 
 def forwards(phase, piece, source):
@@ -61,7 +61,7 @@
             yield "-", (phase, piece, (0, 1))
 
 
-def schedule(rate=43.5e3, lag=1.0, lead=10.0, step=0.05):
+def schedule(rate=41e3, lag=3.0, lead=10.0, step=0.05):
     spent = (None, 1.1, 0.7)
     waiting = {link: [] for link in "+-z"}
     for order, (link, message) in enumerate(own_sends()):

time: 152 us -> 146 us (0.961)
  Pallas kernels: 148 us -> 141 us
    pallas_call x1, Pallas kernels: 148 us -> 141 us  [fused(): pl.pallas_call(functools.partial(kernel, ops), out_shape=(pltpu.VMEM((4,...]
where the time goes in v5:
time: 146 us; the launch traced here: 144 us
  Pallas kernels  141 us (97%)
  local copies, waits for them, and re-layouts  1.71 us (1%)
    pallas_call x1, Pallas kernels, fused(): pl.pallas_call(functools.partial(kernel, ops), out_shape=(pltpu.VMEM((4,...  141 us

profile of v5, /device:TPU:9, one launch (start us, length us, event | category | flops | bytes accessed | tf_op | source)
XLA Modules:
  0.0 143.5 jit_solution(4196784473946828847)
XLA Ops:
  0.6 141.2 %shard_map.77 = (bf16[4,128,384]{2,1,0:T(8,128)(2,1)S(1)}, f32[128,256]{1,0:T(8,128)S(1)}) custom-call(bf16[192,4,384]{2,1,0:T(4,128)(2,1)} %w_ref.1, bf16[1024,3072]{1,0:T(8,128)(2,1)} %bitcast.6, bf16[8,192,384]{2,1,0:T(8,128)(2,1)} %bitcast.7, f32[8,2,2,8]{3,2,1,0:T(2,128)} %bitcast.8, f32[8,2,2,8]{3,2,1,0:T(2,128)} %bitcast.9, s32[16]{0:T(128)} %sector_ref.1), custom_call_target="tpu_custom_call" | custom-call | tf_op jit(solution)/shard_map/pallas_call | solution.py:617
  141.8 1.1 copy.8
  142.9 0.7 copy.10

commit v6 on v5

--- a/solution.py
+++ b/solution.py
@@ -479,7 +479,7 @@
         )
 
     def reach():
-        for offset in (0, *OFFSETS):
+        for offset in (0, *OFFSETS[3:], *OFFSETS[:3]):
             half, at = int(offset < 0), abs(offset) - 1
 
             @pl.when(inside(here + offset))

time: 146 us -> 144 us (0.986); the launches traced: 144 us -> 143 us
  no operation moved by 1% of the time
where the time goes in v6:
time: 144 us; the launch traced here: 143 us
  Pallas kernels  141 us (98%)
  local copies, waits for them, and re-layouts  1.71 us (1%)
    pallas_call x1, Pallas kernels, fused(): pl.pallas_call(functools.partial(kernel, ops), out_shape=(pltpu.VMEM((4,...  141 us

profile of v6, /device:TPU:9, one launch (start us, length us, event | category | flops | bytes accessed | tf_op | source)
XLA Modules:
  0.0 143.4 jit_solution(3818338867372198729)
XLA Ops:
  0.6 141.0 %shard_map.77 = (bf16[4,128,384]{2,1,0:T(8,128)(2,1)S(1)}, f32[128,256]{1,0:T(8,128)S(1)}) custom-call(bf16[192,4,384]{2,1,0:T(4,128)(2,1)} %w_ref.1, bf16[1024,3072]{1,0:T(8,128)(2,1)} %bitcast.6, bf16[8,192,384]{2,1,0:T(8,128)(2,1)} %bitcast.7, f32[8,2,2,8]{3,2,1,0:T(2,128)} %bitcast.8, f32[8,2,2,8]{3,2,1,0:T(2,128)} %bitcast.9, s32[16]{0:T(128)} %sector_ref.1), custom_call_target="tpu_custom_call" | custom-call | tf_op jit(solution)/shard_map/pallas_call | solution.py:617
  141.7 1.1 copy.8
  142.7 0.7 copy.10
